TPU v7x, 32 devices: a whole 2x2x4 slice. The times are simulated.
32 devices in a mesh: groups: 2 (over x), tx: 16 (over z, y, core).
Axes of the slice: x: 2, y: 2, z: 4, core: 2. Of those that a mesh axis runs over, the one named last changes fastest.
Arguments:
- masters: float32 [128, 1024], P(('groups', 'tx')), parts along dimension 0, may hold values from 0 to 1
- velocity: float32 [128, 1024], P(('groups', 'tx')), parts along dimension 0, may hold values from -4 to 4
- place_owner: int32 [4096, 1], P(('groups', 'tx')), parts along dimension 0, may hold values from 0 to 15; in each aligned block of 128 rows (0 to 127, 128 to 255, ...) at most 16 rows name the same one
- place_local: int32 [4096], P(('groups', 'tx')), parts along dimension 0, may hold values from 0 to 3
- place_row: int32 [4096], P(('groups', 'tx')), parts along dimension 0, may hold values from 0 to 32
- place_col: int32 [4096], P(('groups', 'tx')), parts along dimension 0, may hold values from 0 to 224
- row_taps: bfloat16 [12, 4, 2, 63], replicated, may hold values from -0.75 to 0.75
- col_taps: bfloat16 [12, 4, 2, 63], replicated, may hold values from -0.25 to 0.25
- mode_weights: float32 [12], replicated, may hold values from 0.02 to 0.2
- target: bfloat16 [2048, 256], P(('groups', 'tx')), parts along dimension 0, may hold values from 0 to 1
Outputs:
- resist_residual: float32 [2048, 256], P(('groups', 'tx')), parts along dimension 0
- velocity_new: float32 [128, 1024], P(('groups', 'tx')), parts along dimension 0
- masters_new: float32 [128, 1024], P(('groups', 'tx')), parts along dimension 0
There are 2 independent parts, one for each index of `groups`. A program takes and returns all parts, laid end to end along the dimension named above; an argument that names none is the same for every part. Nothing has to cross between parts.
Inputs may be any that keep to these rules, and one draw needn't show every extreme that they name: `place_owner`: among the placements of one device (aligned blocks of 128), at most 16 name any one owner, a bound that some block reaches.
All inputs are finite; a program needn't handle non-finite values.
Results may differ from a plain program's by a relative error of at most 0.0012.
Values may be sent and summed in bfloat16 or wider, within the bound.
A program may use at most 192 MiB of HBM per device.

v0:
```python
import jax
import jax.numpy as jnp
from jax import lax
from jax.sharding import PartitionSpec as P

W = 256
MS = 32
TAPS = 63
HALF = 31
TERMS = 4
MODES = 12


steepness = 0.5
threshold = 8.0
momentum = 0.9
step_size = 0.05


def extended(block, sides, width):
    for axis, dim in sides:
        count = lax.axis_size(axis)
        forward = [(i, i + 1) for i in range(count - 1)]
        backward = [(target, source) for source, target in forward]
        low = lax.ppermute(
            lax.slice_in_dim(block, block.shape[dim] - width, None, axis=dim), axis, forward
        )
        high = lax.ppermute(lax.slice_in_dim(block, 0, width, axis=dim), axis, backward)
        block = jnp.concatenate([low, block, high], axis=dim)
    return block


def from_behind(value, axis, steps):
    count = lax.axis_size(axis)
    initial, last = (max(0, -steps), min(count, count - steps))
    return lax.ppermute(value, axis, [(source, source + steps) for source in range(initial, last)])


def all_row_bands(row_taps, rows_here):
    out_rows = jnp.arange(rows_here, dtype=jnp.int32)
    in_rows = jnp.arange(rows_here + 2 * HALF, dtype=jnp.int32)
    tap_iota = jnp.arange(TAPS, dtype=jnp.int32)
    picker = (in_rows[None, :, None] - out_rows[:, None, None] == tap_iota[None, None, :]).astype(
        jnp.bfloat16
    )
    filters = row_taps.reshape(MODES, 2 * TERMS, TAPS)
    return jnp.einsum("kct,rst->kcrs", filters, picker, preferred_element_type=jnp.float32).astype(
        jnp.bfloat16
    )


def all_column_bands(col_taps):
    cells = jnp.arange(W, dtype=jnp.int32)
    tap_iota = jnp.arange(TAPS, dtype=jnp.int32)
    picker = (cells[:, None, None] - cells[None, :, None] + HALF == tap_iota[None, None, :]).astype(
        jnp.bfloat16
    )
    bands = jnp.einsum(
        "kxpt,wot->kxpwo", col_taps, picker, preferred_element_type=jnp.float32
    ).astype(jnp.bfloat16)
    real_band = bands[:, :, 0]
    imag_band = bands[:, :, 1]
    from_real = jnp.concatenate([real_band, imag_band], axis=-1)
    from_imag = jnp.concatenate([-imag_band, real_band], axis=-1)
    return jnp.stack([from_real, from_imag], axis=2).reshape(MODES, 2 * TERMS, W, 2 * W)


def on_device(
    masters,
    velocity,
    place_owner,
    place_local,
    place_row,
    place_col,
    row_taps,
    col_taps,
    mode_weights,
    target,
):
    rows_here = target.shape[0]
    places = place_local.shape[0]
    owners_count = lax.axis_size("tx")
    owner_dev = place_owner[:, 0]
    master_half = masters.astype(jnp.bfloat16)
    master_count = masters.shape[0]
    offsets = jnp.arange(MS, dtype=jnp.int32)
    row_chosen = (
        place_row[:, None, None] + offsets[None, :, None]
        == jnp.arange(rows_here, dtype=jnp.int32)[None, None, :]
    )
    col_chosen = (
        place_col[:, None, None] + offsets[None, :, None]
        == jnp.arange(W, dtype=jnp.int32)[None, None, :]
    )
    capacity = 2 * places // owners_count
    place_iota = jnp.arange(places, dtype=jnp.int32)
    same_owner = (owner_dev[:, None] == owner_dev[None, :]) & (
        place_iota[None, :] < place_iota[:, None]
    )
    slot_rank = jnp.sum(same_owner.astype(jnp.int32), axis=1)
    slot_index = owner_dev * capacity + slot_rank
    slot_chosen = (
        slot_index[:, None] == jnp.arange(owners_count * capacity, dtype=jnp.int32)[None, :]
    )
    requests = jnp.sum(jnp.where(slot_chosen, (place_local + 1)[:, None], 0), axis=0).reshape(
        owners_count, capacity
    )
    received = lax.all_to_all(requests, "tx", split_axis=0, concat_axis=0, tiled=True)
    lookup = (received[..., None] - 1 == jnp.arange(master_count, dtype=jnp.int32)).astype(
        jnp.bfloat16
    )
    replies = jnp.einsum(
        "scm,mf->scf", lookup, master_half, preferred_element_type=jnp.float32
    ).astype(jnp.bfloat16)
    replies, asked = (replies, received)
    returned = lax.all_to_all(replies, "tx", split_axis=0, concat_axis=0, tiled=True)
    patterns = jnp.dot(
        slot_chosen.astype(jnp.bfloat16),
        returned.reshape(owners_count * capacity, MS * MS),
        preferred_element_type=jnp.float32,
    )
    pattern_half = patterns.reshape(places, MS, MS).astype(jnp.bfloat16)
    spread = jnp.einsum(
        "pab,pbj->paj",
        pattern_half,
        col_chosen.astype(jnp.bfloat16),
        preferred_element_type=jnp.float32,
    ).astype(jnp.bfloat16)
    mask = jnp.einsum(
        "pai,paj->ij", row_chosen.astype(jnp.bfloat16), spread, preferred_element_type=jnp.float32
    ).astype(jnp.bfloat16)
    padded_mask = extended(mask, (("tx", 0),), HALF)
    row_stack = all_row_bands(row_taps, rows_here)
    column_stack = all_column_bands(col_taps)

    def forward_mode(running, pair):
        row_band, column_band = pair
        field_y = jnp.einsum(
            "crs,sw->crw", row_band, padded_mask, preferred_element_type=jnp.float32
        ).astype(jnp.bfloat16)
        field_e = jnp.einsum(
            "crw,cwo->ro", field_y, column_band, preferred_element_type=jnp.float32
        )
        return (running, field_e)

    _, fields = lax.scan(forward_mode, jnp.zeros((), jnp.float32), (row_stack, column_stack))
    field_re = fields[:, :, :W]
    field_im = fields[:, :, W:]
    intensity = jnp.sum(
        mode_weights[:, None, None] * (field_re * field_re + field_im * field_im), 0
    )
    resist = jax.nn.sigmoid(steepness * (intensity - threshold))
    resist_residual = resist - target.astype(jnp.float32)
    grad_intensity = resist_residual * steepness * resist * (1.0 - resist)
    doubled = jnp.concatenate([grad_intensity, grad_intensity], axis=-1)
    grad_fields = (2.0 * mode_weights[:, None, None] * doubled[None] * fields).astype(jnp.bfloat16)

    def adjoint_mode(running, inputs):
        row_band, column_band, grad_field = inputs
        grad_y = jnp.einsum(
            "ro,cwo->crw", grad_field, column_band, preferred_element_type=jnp.float32
        ).astype(jnp.bfloat16)
        return (
            running
            + jnp.einsum("crs,crw->sw", row_band, grad_y, preferred_element_type=jnp.float32),
            None,
        )

    grad_padded, _ = lax.scan(
        adjoint_mode,
        jnp.zeros((rows_here + 2 * HALF, W), jnp.float32),
        (row_stack, column_stack, grad_fields),
    )
    top_rim = grad_padded[:HALF]
    bottom_rim = grad_padded[HALF + rows_here :]
    from_above = from_behind(bottom_rim, "tx", 1)
    from_below = from_behind(top_rim, "tx", -1)
    grad_mask = grad_padded[HALF : HALF + rows_here]
    grad_mask = grad_mask + jnp.pad(from_above, ((0, rows_here - HALF), (0, 0)))
    grad_mask = grad_mask + jnp.pad(from_below, ((rows_here - HALF, 0), (0, 0)))
    row_rows = jnp.einsum(
        "pai,ij->paj", row_chosen.astype(jnp.float32), grad_mask, precision=lax.Precision.HIGHEST
    )
    grad_patch = jnp.einsum(
        "paj,pcj->pac", row_rows, col_chosen.astype(jnp.float32), precision=lax.Precision.HIGHEST
    ).reshape(places, MS * MS)
    slot_grads = jnp.dot(
        slot_chosen.astype(jnp.float32).T, grad_patch, precision=lax.Precision.HIGHEST
    ).reshape(owners_count, capacity, MS * MS)
    arrived = lax.all_to_all(slot_grads, "tx", split_axis=0, concat_axis=0, tiled=True)
    lookup = (
        asked.reshape(-1)[None, :] - 1 == jnp.arange(master_count, dtype=jnp.int32)[:, None]
    ).astype(jnp.float32)
    master_grad = jnp.dot(
        lookup, arrived.reshape(owners_count * capacity, MS * MS), precision=lax.Precision.HIGHEST
    )
    velocity_new = momentum * velocity + master_grad
    masters_new = masters - step_size * velocity_new
    return (resist_residual, velocity_new, masters_new)


def solution(mesh):
    return jax.shard_map(
        on_device,
        mesh=mesh,
        in_specs=(
            P(("groups", "tx"), None),
            P(("groups", "tx"), None),
            P(("groups", "tx"), None),
            P(("groups", "tx")),
            P(("groups", "tx")),
            P(("groups", "tx")),
            P(),
            P(),
            P(),
            P(("groups", "tx"), None),
        ),
        out_specs=(P(("groups", "tx"), None), P(("groups", "tx"), None), P(("groups", "tx"), None)),
        check_vma=False,
    )
```

profile of v0, /device:TPU:1, one launch (start us, length us, event | category | flops | bytes accessed | tf_op | source)
XLA Modules:
  0.0 255.1 jit_solution(10167865873663665052)
XLA Ops:
  3.7 7.3 %all-to-all-start = ((s32[16,1,16]{2,1,0:T(1,128)}), s32[16,1,16]{2,1,0:T(1,128)S(1)}, u32[]{:S(2)}, u32[]{:S(2)}) async-start(s32[16,1,16]{2,1,0:T(1,128)} %all_to_all.12), calls=%async_computation | async-start | bytes 16384 | tf_op jit(solution)/shard_map/all_to_all | solution.py:108
  11.1 8.9 %convert_bitcast_fusion = bf16[12,4,2,256,256]{4,0,2,1,3:T(8,128)(2,1)} fusion(s32[256,256]{1,0:T(8,128)S(1)} %subtract_add_fusion, bf16[12,4,2,63]{3,2,1,0:T(2,128)(2,1)} %param.21), kind=kOutput, calls=%fused_computation.26 | convolution fusion | flops 803143680 | bytes 12857152 | tf_op jit(solution)/shard_map/kxpt,wot->kxpwo/dot_general | solution.py:58
  20.0 12.0 %slice_bitcast_fusion = (bf16[12,4,256,256]{3,0,1,2:T(8,128)(2,1)}, bf16[12,4,256,256]{3,0,1,2:T(8,128)(2,1)}) fusion(bf16[12,4,2,256,256]{4,0,2,1,3:T(8,128)(2,1)} %convert_bitcast_fusion), kind=kLoop, calls=%fused_computation.30 | loop fusion | bytes 25165824 | tf_op jit(solution)/shard_map/squeeze | solution.py:62
  32.0 7.2 %fusion.96 = bf16[12,4,256,256]{3,0,1,2:T(8,128)(2,1)} fusion(bf16[12,4,2,256,256]{4,0,2,1,3:T(8,128)(2,1)} %convert_bitcast_fusion), kind=kLoop, calls=%fused_computation.101 | loop fusion | flops 3145728 | bytes 12582912 | tf_op jit(solution)/shard_map/neg | solution.py:64
  39.9 25.1 %maximum_bitcast_fusion = (bf16[12,4,1,256,512]{4,0,1,3,2:T(8,128)(2,1)}, bf16[12,4,1,256,512]{4,0,1,3,2:T(8,128)(2,1)}) fusion(bf16[12,4,256,256]{3,0,1,2:T(8,128)(2,1)} %get-tuple-element.139, bf16[12,4,256,256]{3,0,1,2:T(8,128)(2,1)} %get-tuple-element.140, bf16[12,4,256,256]{3,0,1,2:T(8,128)(2,1)} %fusion.96), kind=kLoop, calls=%fused_computation.24 | loop fusion | flops 50331648 | bytes 44040192 | tf_op jit(solution)/shard_map/stack | solution.py:65
  67.0 6.0 %all-to-all-start.1 = ((bf16[16,16,1024]{2,1,0:T(8,128)(2,1)}), bf16[16,16,1024]{2,1,0:T(8,128)(2,1)S(1)}, u32[]{:S(2)}, u32[]{:S(2)}) async-start(bf16[16,16,1024]{2,1,0:T(8,128)(2,1)} %convolution_convert_fusion.1), calls=%async_computation.1 | async-start | bytes 1048576 | tf_op jit(solution)/shard_map/all_to_all | solution.py:116
  73.0 22.5 %pad_maximum_fusion = bf16[12,4,2,256,512]{4,0,1,3,2:T(8,128)(2,1)} fusion(bf16[12,4,1,256,512]{4,0,1,3,2:T(8,128)(2,1)} %get-tuple-element.142, bf16[12,4,1,256,512]{4,0,1,3,2:T(8,128)(2,1)} %get-tuple-element.141), kind=kLoop, calls=%fused_computation.23 | loop fusion | flops 12582912 | bytes 50331648 | tf_op jit(solution)/shard_map/stack | solution.py:65
  100.2 3.5 %collective-permute-start = (bf16[31,256]{1,0:T(8,128)(2,1)S(1)}, bf16[31,256]{1,0:T(8,128)(2,1)S(1)}, u32[]{:S(2)}, u32[]{:S(2)}) collective-permute-start(bf16[31,256]{1,0:T(8,128)(2,1)S(1)} %get-tuple-element.145), channel_id=1, source_target_pairs={{0,1},{1,2},{2,3},{3,4},{4,5},{5,6},{6,7},{7,8},{8,9},{9,10},{10,1... | collective-permute-start | bytes 47624 | tf_op jit(solution)/shard_map/ppermute | solution.py:25
  106.5 28.4 %copy.44 = bf16[12,4,2,256,512]{4,3,2,1,0:T(8,128)(2,1)} copy(bf16[12,4,2,256,512]{4,0,1,3,2:T(8,128)(2,1)} %pad_maximum_fusion) | data formatting | bytes 50331648 | tf_op jit(solution)/shard_map/stack | solution.py:65
  137.1 34.9 %while.21 = (s32[]{:T(128)}, f32[12,64,512]{2,1,0:T(8,128)}, bf16[12,8,64,126]{3,2,1,0:T(8,128)(2,1)}, bf16[126,256]{1,0:T(8,128)(2,1)S(1)}, bf16[12,8,256,512]{3,2,1,0:T(8,128)(2,1)}, /*index=5*/s32[]{:T(128)}) while((s32[]{:T(128)}, f32[12,64,512]{2,1,0:T(8,128)}, bf16[12,8,64,126]{3,2,1,0:T(8,128)(2,1)}, bf16[126,256]{1,0:T(8,128)(2,1)S(1)}, ...), condition=%wide.region_3.4_spmd, body=%wide.region_2.3_spmd.sunk | while | flops 167378944 | bytes 2425413 | solution.py:146
  137.1 2.9 %fusion.115 = f32[12,64,512]{2,1,0:T(8,128)} fusion(f32[12,64,512]{2,1,0:T(8,128)} %get-tuple-element.222, s32[]{:T(128)} %get-tuple-element.221, bf16[12,8,256,512]{3,2,1,0:T(8,128)(2,1)} %get-tuple-element.231, bf16[12,8,64,126]{3,2,1,0:T(8,128)(2,1)} %get-tuple-element.229, bf16[126,256]{1,0:T(8,128)(2,1)S(1)} %get-tuple-element.230), kind=kOutput, calls=%fused_computation.5.clone.1 | convolution fusion | flops 167378944 | bytes 2425344 | tf_op jit(solution)/shard_map/while/body/eval_jaxpr/crw,cwo->ro/dot_general | solution.py:141
  148.8 2.9 %fusion.115 = f32[12,64,512]{2,1,0:T(8,128)} fusion(f32[12,64,512]{2,1,0:T(8,128)} %get-tuple-element.222, s32[]{:T(128)} %get-tuple-element.221, bf16[12,8,256,512]{3,2,1,0:T(8,128)(2,1)} %get-tuple-element.231, bf16[12,8,64,126]{3,2,1,0:T(8,128)(2,1)} %get-tuple-element.229, bf16[126,256]{1,0:T(8,128)(2,1)S(1)} %get-tuple-element.230), kind=kOutput, calls=%fused_computation.5.clone.1 | convolution fusion | flops 167378944 | bytes 2425344 | tf_op jit(solution)/shard_map/while/body/eval_jaxpr/crw,cwo->ro/dot_general | solution.py:141
  151.7 2.9 %fusion.115 = f32[12,64,512]{2,1,0:T(8,128)} fusion(f32[12,64,512]{2,1,0:T(8,128)} %get-tuple-element.222, s32[]{:T(128)} %get-tuple-element.221, bf16[12,8,256,512]{3,2,1,0:T(8,128)(2,1)} %get-tuple-element.231, bf16[12,8,64,126]{3,2,1,0:T(8,128)(2,1)} %get-tuple-element.229, bf16[126,256]{1,0:T(8,128)(2,1)S(1)} %get-tuple-element.230), kind=kOutput, calls=%fused_computation.5.clone.1 | convolution fusion | flops 167378944 | bytes 2425344 | tf_op jit(solution)/shard_map/while/body/eval_jaxpr/crw,cwo->ro/dot_general | solution.py:141
  154.6 2.9 %fusion.115 = f32[12,64,512]{2,1,0:T(8,128)} fusion(f32[12,64,512]{2,1,0:T(8,128)} %get-tuple-element.222, s32[]{:T(128)} %get-tuple-element.221, bf16[12,8,256,512]{3,2,1,0:T(8,128)(2,1)} %get-tuple-element.231, bf16[12,8,64,126]{3,2,1,0:T(8,128)(2,1)} %get-tuple-element.229, bf16[126,256]{1,0:T(8,128)(2,1)S(1)} %get-tuple-element.230), kind=kOutput, calls=%fused_computation.5.clone.1 | convolution fusion | flops 167378944 | bytes 2425344 | tf_op jit(solution)/shard_map/while/body/eval_jaxpr/crw,cwo->ro/dot_general | solution.py:141
  157.5 2.9 %fusion.115 = f32[12,64,512]{2,1,0:T(8,128)} fusion(f32[12,64,512]{2,1,0:T(8,128)} %get-tuple-element.222, s32[]{:T(128)} %get-tuple-element.221, bf16[12,8,256,512]{3,2,1,0:T(8,128)(2,1)} %get-tuple-element.231, bf16[12,8,64,126]{3,2,1,0:T(8,128)(2,1)} %get-tuple-element.229, bf16[126,256]{1,0:T(8,128)(2,1)S(1)} %get-tuple-element.230), kind=kOutput, calls=%fused_computation.5.clone.1 | convolution fusion | flops 167378944 | bytes 2425344 | tf_op jit(solution)/shard_map/while/body/eval_jaxpr/crw,cwo->ro/dot_general | solution.py:141
  160.4 2.9 %fusion.115 = f32[12,64,512]{2,1,0:T(8,128)} fusion(f32[12,64,512]{2,1,0:T(8,128)} %get-tuple-element.222, s32[]{:T(128)} %get-tuple-element.221, bf16[12,8,256,512]{3,2,1,0:T(8,128)(2,1)} %get-tuple-element.231, bf16[12,8,64,126]{3,2,1,0:T(8,128)(2,1)} %get-tuple-element.229, bf16[126,256]{1,0:T(8,128)(2,1)S(1)} %get-tuple-element.230), kind=kOutput, calls=%fused_computation.5.clone.1 | convolution fusion | flops 167378944 | bytes 2425344 | tf_op jit(solution)/shard_map/while/body/eval_jaxpr/crw,cwo->ro/dot_general | solution.py:141
  166.3 2.9 %fusion.115 = f32[12,64,512]{2,1,0:T(8,128)} fusion(f32[12,64,512]{2,1,0:T(8,128)} %get-tuple-element.222, s32[]{:T(128)} %get-tuple-element.221, bf16[12,8,256,512]{3,2,1,0:T(8,128)(2,1)} %get-tuple-element.231, bf16[12,8,64,126]{3,2,1,0:T(8,128)(2,1)} %get-tuple-element.229, bf16[126,256]{1,0:T(8,128)(2,1)S(1)} %get-tuple-element.230), kind=kOutput, calls=%fused_computation.5.clone.1 | convolution fusion | flops 167378944 | bytes 2425344 | tf_op jit(solution)/shard_map/while/body/eval_jaxpr/crw,cwo->ro/dot_general | solution.py:141
  169.2 2.9 %fusion.115 = f32[12,64,512]{2,1,0:T(8,128)} fusion(f32[12,64,512]{2,1,0:T(8,128)} %get-tuple-element.222, s32[]{:T(128)} %get-tuple-element.221, bf16[12,8,256,512]{3,2,1,0:T(8,128)(2,1)} %get-tuple-element.231, bf16[12,8,64,126]{3,2,1,0:T(8,128)(2,1)} %get-tuple-element.229, bf16[126,256]{1,0:T(8,128)(2,1)S(1)} %get-tuple-element.230), kind=kOutput, calls=%fused_computation.5.clone.1 | convolution fusion | flops 167378944 | bytes 2425344 | tf_op jit(solution)/shard_map/while/body/eval_jaxpr/crw,cwo->ro/dot_general | solution.py:141
  176.0 31.6 %while.22 = (s32[]{:T(128)}, f32[126,256]{1,0:T(8,128)S(1)}, bf16[12,8,64,126]{3,2,1,0:T(8,128)(2,1)}, bf16[12,8,256,512]{3,2,1,0:T(8,128)(2,1)}, bf16[12,64,512]{2,1,0:T(8,128)(2,1)S(1)}, /*index=5*/s32[]{:T(128)}, s32[]{:T(128)}) while((s32[]{:T(128)}, f32[126,256]{1,0:T(8,128)S(1)}, bf16[12,8,64,126]{3,2,1,0:T(8,128)(2,1)}, ...), condition=%wide.region_6.7_spmd.clone, body=%wide.region_5.6_spmd.clone.sunk | while | flops 167443456 | bytes 2555479 | solution.py:169
  207.6 3.6 %collective-permute-start.2 = (f32[31,256]{1,0:T(8,128)S(1)}, f32[31,256]{1,0:T(8,128)S(1)}, u32[]{:S(2)}, u32[]{:S(2)}) collective-permute-start(f32[31,256]{1,0:T(8,128)S(1)} %get-tuple-element.143), channel_id=1, source_target_pairs={{0,1},{1,2},{2,3},{3,4},{4,5},{5,6},{6,7},{7,8},{8,9},{9,10},{10,1... | collective-permute-start | bytes 95240 | tf_op jit(solution)/shard_map/ppermute | solution.py:36
  213.2 3.3 %collective-permute-done.3 = f32[31,256]{1,0:T(8,128)S(1)} collective-permute-done((f32[31,256]{1,0:T(8,128)S(1)}, f32[31,256]{1,0:T(8,128)S(1)}, u32[]{:S(2)}, u32[]{:S(2)}) %collective-permute-start.3) | collective-permute-done | bytes 31776 | tf_op jit(solution)/shard_map/ppermute | solution.py:36
  218.4 3.1 %fusion.49 = f32[128,32,32]{2,1,0:T(8,128)S(1)} fusion(f32[128,32,256]{2,1,0:T(8,128)S(1)} %fusion.56, s32[128,32]{1,0:T(8,128)S(1)} %get-tuple-element.151), kind=kOutput, calls=%fused_computation.34 | convolution fusion | flops 403701760 | bytes 4734976 | tf_op jit(solution)/shard_map/paj,pcj->pac/dot_general | solution.py:184
  224.4 6.5 %all-to-all-start.2 = ((f32[16,16,1024]{2,1,0:T(8,128)}), f32[16,16,1024]{2,1,0:T(8,128)S(1)}, u32[]{:S(2)}, u32[]{:S(2)}) async-start(f32[16,16,1024]{2,1,0:T(8,128)} %fusion.73), calls=%async_computation.2 | async-start | bytes 2097152 | tf_op jit(solution)/shard_map/all_to_all | solution.py:190
  231.0 23.1 %all-to-all-done.2 = f32[16,16,1024]{2,1,0:T(8,128)S(1)} async-done(((f32[16,16,1024]{2,1,0:T(8,128)}), f32[16,16,1024]{2,1,0:T(8,128)S(1)}, u32[]{:S(2)}, u32[]{:S(2)}) %all-to-all-start.2) | async-done | bytes 1048608 | tf_op jit(solution)/shard_map/all_to_all | solution.py:190
  (75 shorter events, 70.0 us)
Async XLA Ops:
  2.2 0.7 copy-start.5
  3.7 61.5 %all-to-all-start = ((s32[16,1,16]{2,1,0:T(1,128)}), s32[16,1,16]{2,1,0:T(1,128)S(1)}, u32[]{:S(2)}, u32[]{:S(2)}) async-start(s32[16,1,16]{2,1,0:T(1,128)} %all_to_all.12), calls=%async_computation | async-start | bytes 16384 | tf_op jit(solution)/shard_map/all_to_all | solution.py:108
  32.0 7.2 %copy-start.1 = (bf16[12,4,2,63]{3,2,1,0:T(2,128)(2,1)S(1)}, bf16[12,4,2,63]{3,2,1,0:T(2,128)(2,1)}, u32[]{:S(2)}) copy-start(bf16[12,4,2,63]{3,2,1,0:T(2,128)(2,1)} %param.20) | copy-start | bytes 36292
  39.9 25.2 %copy-start.7 = (s32[128]{0:T(128)S(1)}, s32[128]{0:T(128)}, u32[]{:S(2)}) copy-start(s32[128]{0:T(128)} %param.19) | copy-start | bytes 1540
  39.9 25.2 %copy-start.8 = (s32[128]{0:T(128)S(1)}, s32[128]{0:T(128)}, u32[]{:S(2)}) copy-start(s32[128]{0:T(128)} %param.18) | copy-start | bytes 1540
  39.9 25.9 %copy-start = (f32[4,1024]{1,0:T(4,128)S(1)}, f32[4,1024]{1,0:T(4,128)}, u32[]{:S(2)}) copy-start(f32[4,1024]{1,0:T(4,128)} %param.14) | copy-start | bytes 49156
  67.0 28.5 %all-to-all-start.1 = ((bf16[16,16,1024]{2,1,0:T(8,128)(2,1)}), bf16[16,16,1024]{2,1,0:T(8,128)(2,1)S(1)}, u32[]{:S(2)}, u32[]{:S(2)}) async-start(bf16[16,16,1024]{2,1,0:T(8,128)(2,1)} %convolution_convert_fusion.1), calls=%async_computation.1 | async-start | bytes 1048576 | tf_op jit(solution)/shard_map/all_to_all | solution.py:116
  100.2 36.9 %collective-permute-start = (bf16[31,256]{1,0:T(8,128)(2,1)S(1)}, bf16[31,256]{1,0:T(8,128)(2,1)S(1)}, u32[]{:S(2)}, u32[]{:S(2)}) collective-permute-start(bf16[31,256]{1,0:T(8,128)(2,1)S(1)} %get-tuple-element.145), channel_id=1, source_target_pairs={{0,1},{1,2},{2,3},{3,4},{4,5},{5,6},{6,7},{7,8},{8,9},{9,10},{10,1... | collective-permute-start | bytes 47624 | tf_op jit(solution)/shard_map/ppermute | solution.py:25
  103.7 33.4 %collective-permute-start.1 = (bf16[31,256]{1,0:T(8,128)(2,1)S(1)}, bf16[31,256]{1,0:T(8,128)(2,1)S(1)}, u32[]{:S(2)}, u32[]{:S(2)}) collective-permute-start(bf16[31,256]{1,0:T(8,128)(2,1)S(1)} %get-tuple-element.146), channel_id=1, source_target_pairs={{1,0},{2,1},{3,2},{4,3},{5,4},{6,5},{7,6},{8,7},{9,8},{10,9},{11,1... | collective-permute-start | bytes 47624 | tf_op jit(solution)/shard_map/ppermute | solution.py:28
  137.1 35.0 %copy-start.9 = (f32[12]{0:T(128)S(1)}, f32[12]{0:T(128)}, u32[]{:S(2)}) copy-start(f32[12]{0:T(128)} %param.22) | copy-start | bytes 148
  137.1 36.5 %copy-start.2 = (bf16[64,256]{1,0:T(8,128)(2,1)S(1)}, bf16[64,256]{1,0:T(8,128)(2,1)}, u32[]{:S(2)}) copy-start(bf16[64,256]{1,0:T(8,128)(2,1)} %param.23) | copy-start | bytes 98308
  207.6 5.6 %collective-permute-start.2 = (f32[31,256]{1,0:T(8,128)S(1)}, f32[31,256]{1,0:T(8,128)S(1)}, u32[]{:S(2)}, u32[]{:S(2)}) collective-permute-start(f32[31,256]{1,0:T(8,128)S(1)} %get-tuple-element.143), channel_id=1, source_target_pairs={{0,1},{1,2},{2,3},{3,4},{4,5},{5,6},{6,7},{7,8},{8,9},{9,10},{10,1... | collective-permute-start | bytes 95240 | tf_op jit(solution)/shard_map/ppermute | solution.py:36
  211.3 5.2 %collective-permute-start.3 = (f32[31,256]{1,0:T(8,128)S(1)}, f32[31,256]{1,0:T(8,128)S(1)}, u32[]{:S(2)}, u32[]{:S(2)}) collective-permute-start(f32[31,256]{1,0:T(8,128)S(1)} %get-tuple-element.144), channel_id=1, source_target_pairs={{1,0},{2,1},{3,2},{4,3},{5,4},{6,5},{7,6},{8,7},{9,8},{10,9},{11,1... | collective-permute-start | bytes 95240 | tf_op jit(solution)/shard_map/ppermute | solution.py:36
  218.4 4.4 %copy-start.6 = (s32[128]{0:T(128)S(1)}, s32[128]{0:T(128)}, u32[]{:S(2)}) copy-start(s32[128]{0:T(128)} %copy-done.5) | copy-start | bytes 1540
  221.5 9.4 %copy-start.3 = (s32[16,16]{1,0:T(8,128)S(1)}, s32[16,16]{1,0:T(8,128)}, u32[]{:S(2)}) copy-start(s32[16,16]{1,0:T(8,128)} %get-tuple-element.147) | copy-start | bytes 3076
  221.6 32.5 %copy-start.4 = (f32[4,1024]{1,0:T(4,128)S(1)}, f32[4,1024]{1,0:T(4,128)}, u32[]{:S(2)}) copy-start(f32[4,1024]{1,0:T(4,128)} %param.15) | copy-start | bytes 49156
  224.4 29.6 %all-to-all-start.2 = ((f32[16,16,1024]{2,1,0:T(8,128)}), f32[16,16,1024]{2,1,0:T(8,128)S(1)}, u32[]{:S(2)}, u32[]{:S(2)}) async-start(f32[16,16,1024]{2,1,0:T(8,128)} %fusion.73), calls=%async_computation.2 | async-start | bytes 2097152 | tf_op jit(solution)/shard_map/all_to_all | solution.py:190
where the time goes:
time: 258 us; the launch traced here: 255 us
  matrix products  87.7 us (34%)
  other arithmetic  62.5 us (24%)
  local copies, waits for them, and re-layouts  46.4 us (18%)
  starting transfers between devices  31 us (12%)
  waiting for transfers between devices  26.3 us (10%)
    another operation x2, other arithmetic, all_column_bands(): jnp.stack([from_real, from_imag], axis=2)  47.6 us
    dot_general x12, matrix products, forward_mode(): jnp.einsum('crw,cwo->ro', field_y, column_band, preferred_element_type=jn...  34.9 us
    dot_general x12, matrix products, adjoint_mode(): jnp.einsum('crs,crw->sw', row_band, grad_y, preferred_element_type=jnp.fl...  31.3 us
    another operation x1, local copies, waits for them, and re-layouts, all_column_bands(): jnp.stack([from_real, from_imag], axis=2)  28.4 us
    all_to_all x1, waiting for transfers between devices, on_device(): lax.all_to_all(slot_grads, 'tx', split_axis=0, concat_axis=0, tiled=True)  23.1 us
    squeeze x1, local copies, waits for them, and re-layouts, all_column_bands(): imag_band = bands[:, :, 1]  12 us
    dot_general x1, matrix products, all_column_bands(): jnp.einsum('kxpt,wot->kxpwo', col_taps, picker, preferred_element_type=jn...  8.91 us
    all_to_all x1, starting transfers between devices, on_device(): lax.all_to_all(requests, 'tx', split_axis=0, concat_axis=0, tiled=True)  7.35 us
  transfers between devices with their start and end apart: 7, of which 2 were waited for; matrix products, arithmetic and copies ran while one was open for 42% of the time, Pallas kernels for 0%

commit v1 on v0

v1 whole, which is shorter than its diff:
```python
import jax
import jax.numpy as jnp
from jax import lax
from jax.experimental import pallas as pl
from jax.experimental.pallas import tpu as pltpu
from jax.sharding import PartitionSpec as P

W = 256
MS = 32
TAPS = 63
HALF = 31
TERMS = 4
MODES = 12
FILTERS = 2 * TERMS
LANES = 128


steepness = 0.5
threshold = 8.0
momentum = 0.9
step_size = 0.05


def halo(block, axis, width):
    count = lax.axis_size(axis)
    forward = [(i, i + 1) for i in range(count - 1)]
    backward = [(target, source) for source, target in forward]
    low = lax.ppermute(block[-width:], axis, forward)
    high = lax.ppermute(block[:width], axis, backward)
    return low, high


def tap_rows(row_taps, col_taps):
    row = row_taps.reshape(MODES, FILTERS, TAPS).astype(jnp.float32)
    col = col_taps.reshape(MODES, FILTERS, TAPS).astype(jnp.float32)
    rest = LANES - TAPS

    def pad(x, low, high):
        return jnp.pad(x, ((0, 0), (0, 0), (low, high)))

    row_fwd = pad(row, 0, rest)
    row_adj = jnp.concatenate([row[..., :1], pad(row[..., :0:-1], rest, 0)], axis=-1)
    col_fwd = pad(col[..., ::-1], rest, 0)
    col_adj = pad(col, rest, 0)
    return row_fwd, row_adj, col_fwd, col_adj


def rolled(taps, rows, shift):
    return pltpu.roll(
        jnp.broadcast_to(taps, (rows, LANES)), shift, 1, stride=1, stride_axis=0
    )


def column_bands(taps):
    row_iota = lax.broadcasted_iota(jnp.int32, (LANES, LANES), 0)
    lane_iota = lax.broadcasted_iota(jnp.int32, (LANES, LANES), 1)
    below = lane_iota < row_iota
    bands = []
    for c in range(FILTERS):
        circle = rolled(taps[c : c + 1], LANES, 0)
        low = jnp.where(below, circle, 0.0)
        high = jnp.where(below, 0.0, circle)
        bands.append(jnp.concatenate([low, high], axis=0))
    return bands


def filters_kernel(
    rows_here, weights_ref, row_fwd_ref, row_adj_ref, col_fwd_ref, col_adj_ref, mask_ref,
    target_ref, residual_ref, grad_ref, fields_ref,
):
    half = jnp.bfloat16
    mask = mask_ref[...]

    def forward_mode(k, intensity):
        row_taps = row_fwd_ref[k]
        row_band = jnp.concatenate(
            [rolled(row_taps[c : c + 1], rows_here, 0).astype(half) for c in range(FILTERS)], axis=0
        )
        field_y = jnp.dot(row_band, mask, preferred_element_type=jnp.float32).astype(half)
        bands = column_bands(col_fwd_ref[k])
        left, right = [], []
        for t in range(TERMS):
            re, im = bands[2 * t], bands[2 * t + 1]
            for p in range(2):
                c = 2 * t + p
                y = field_y[c * rows_here : (c + 1) * rows_here]
                left.append(jnp.concatenate([y[:, : 2 * LANES], y[:, LANES :]], axis=0))
            re_half, im_half = re.astype(half), im.astype(half)
            right.append(jnp.concatenate([re_half, im_half], axis=1))
            right.append(jnp.concatenate([(-im).astype(half), re_half], axis=1))
        field = jnp.dot(
            jnp.concatenate(left, axis=1),
            jnp.concatenate(right, axis=0),
            preferred_element_type=jnp.float32,
        )
        fields_ref[k] = field
        re, im = field[:, :LANES], field[:, LANES:]
        return intensity + weights_ref[k] * (re * re + im * im)

    intensity = lax.fori_loop(
        0, MODES, forward_mode, jnp.zeros((2 * rows_here, LANES), jnp.float32)
    )
    resist = 1.0 / (1.0 + jnp.exp(-(steepness * (intensity - threshold))))
    target = target_ref[...].astype(jnp.float32)
    target = jnp.concatenate([target[:, :LANES], target[:, LANES:]], axis=0)
    residual = resist - target
    residual_ref[:, :LANES] = residual[:rows_here]
    residual_ref[:, LANES:] = residual[rows_here:]
    grad_intensity = residual * steepness * resist * (1.0 - resist)
    grad_ref[...] = jnp.zeros(grad_ref.shape, jnp.float32)

    def adjoint_mode(k, carry):
        field = fields_ref[k]
        scale = (2.0 * weights_ref[k]) * grad_intensity
        windows = []
        for part in range(2):
            g = scale * field[:, part * LANES : (part + 1) * LANES]
            wide = jnp.concatenate(
                [g[:rows_here], g[rows_here:], jnp.zeros((rows_here, LANES), jnp.float32)], axis=1
            )
            wide = pltpu.roll(wide, 32, 1).astype(half)
            windows.append(
                jnp.concatenate([wide[:, : 2 * LANES], wide[:, LANES :]], axis=0)
            )
        bands = column_bands(col_adj_ref[k])
        right = []
        for t in range(TERMS):
            re, im = bands[2 * t], bands[2 * t + 1]
            re_half = re.astype(half)
            right.append(jnp.concatenate([re_half, im.astype(half)], axis=0))
            right.append(jnp.concatenate([(-im).astype(half), re_half], axis=0))
        grad_y = jnp.dot(
            jnp.concatenate(windows, axis=1),
            jnp.concatenate(right, axis=1),
            preferred_element_type=jnp.float32,
        ).astype(half)
        stacked = jnp.concatenate(
            [
                jnp.concatenate(
                    [
                        grad_y[:rows_here, c * LANES : (c + 1) * LANES],
                        grad_y[rows_here:, c * LANES : (c + 1) * LANES],
                    ],
                    axis=1,
                )
                for c in range(FILTERS)
            ],
            axis=0,
        )
        row_taps = row_adj_ref[k]
        first = lax.broadcasted_iota(jnp.int32, (LANES, LANES), 1) < rows_here
        row_band = jnp.concatenate(
            [
                jnp.where(
                    first,
                    rolled(row_taps[2 * t : 2 * t + 1], LANES, 0),
                    rolled(row_taps[2 * t + 1 : 2 * t + 2], LANES, rows_here),
                ).astype(half)
                for t in range(TERMS)
            ],
            axis=1,
        )
        grad_ref[...] += jnp.dot(row_band, stacked, preferred_element_type=jnp.float32)
        return carry

    lax.fori_loop(0, MODES, adjoint_mode, 0)


def run_filters(mask, target, row_taps, col_taps, mode_weights):
    rows_here = target.shape[0]
    vmem = pl.BlockSpec(memory_space=pltpu.VMEM)
    taps = tap_rows(row_taps, col_taps)

    def body(*refs):
        filters_kernel(rows_here, *refs)

    return pl.pallas_call(
        body,
        out_shape=(
            jax.ShapeDtypeStruct((rows_here, W), jnp.float32),
            jax.ShapeDtypeStruct((2 * rows_here, W), jnp.float32),
        ),
        in_specs=[pl.BlockSpec(memory_space=pltpu.SMEM)] + [vmem] * 6,
        out_specs=(vmem, vmem),
        scratch_shapes=[pltpu.VMEM((MODES, 2 * rows_here, W), jnp.float32)],
        compiler_params=pltpu.CompilerParams(vmem_limit_bytes=40 * 1024 * 1024),
        name="filters",
    )(mode_weights, *taps, mask, target)


def on_device(
    masters,
    velocity,
    place_owner,
    place_local,
    place_row,
    place_col,
    row_taps,
    col_taps,
    mode_weights,
    target,
):
    rows_here = target.shape[0]
    places = place_local.shape[0]
    devices = lax.axis_size("tx")
    master_count = masters.shape[0]
    all_masters = lax.all_gather(masters.astype(jnp.bfloat16), "tx", axis=0, tiled=True)
    master_id = place_owner[:, 0] * master_count + place_local
    offsets = jnp.arange(MS, dtype=jnp.int32)
    row_chosen = (
        place_row[:, None, None] + offsets[None, :, None]
        == jnp.arange(rows_here, dtype=jnp.int32)[None, None, :]
    )
    col_chosen = (
        place_col[:, None, None] + offsets[None, :, None]
        == jnp.arange(W, dtype=jnp.int32)[None, None, :]
    )
    chosen = (
        master_id[:, None] == jnp.arange(devices * master_count, dtype=jnp.int32)[None, :]
    )
    pattern_half = (
        jnp.dot(chosen.astype(jnp.bfloat16), all_masters, preferred_element_type=jnp.float32)
        .astype(jnp.bfloat16)
        .reshape(places, MS, MS)
    )
    spread = jnp.einsum(
        "pab,pbj->paj",
        pattern_half,
        col_chosen.astype(jnp.bfloat16),
        preferred_element_type=jnp.float32,
    ).astype(jnp.bfloat16)
    mask = jnp.einsum(
        "pai,paj->ij", row_chosen.astype(jnp.bfloat16), spread, preferred_element_type=jnp.float32
    ).astype(jnp.bfloat16)
    low, high = halo(mask, "tx", HALF)
    padded = jnp.pad(
        jnp.concatenate([low, mask, high], axis=0), ((0, 2 * rows_here - rows_here - 2 * HALF), (32, 96))
    )
    resist_residual, grad_padded = run_filters(padded, target, row_taps, col_taps, mode_weights)
    count = devices
    from_above = lax.ppermute(
        grad_padded[HALF + rows_here : 2 * HALF + rows_here],
        "tx",
        [(i, i + 1) for i in range(count - 1)],
    )
    from_below = lax.ppermute(grad_padded[:HALF], "tx", [(i + 1, i) for i in range(count - 1)])
    grad_mask = grad_padded[HALF : HALF + rows_here]
    grad_mask = grad_mask + jnp.pad(from_above, ((0, rows_here - HALF), (0, 0)))
    grad_mask = grad_mask + jnp.pad(from_below, ((rows_here - HALF, 0), (0, 0)))
    row_rows = jnp.einsum(
        "pai,ij->paj", row_chosen.astype(jnp.float32), grad_mask, precision=lax.Precision.HIGHEST
    )
    grad_patch = jnp.einsum(
        "paj,pcj->pac", row_rows, col_chosen.astype(jnp.float32), precision=lax.Precision.HIGHEST
    ).reshape(places, MS * MS)
    partial = jnp.dot(
        chosen.astype(jnp.float32).T, grad_patch, precision=lax.Precision.HIGHEST
    )
    master_grad = lax.psum_scatter(partial, "tx", scatter_dimension=0, tiled=True)
    velocity_new = momentum * velocity + master_grad
    masters_new = masters - step_size * velocity_new
    return (resist_residual, velocity_new, masters_new)


def solution(mesh):
    return jax.shard_map(
        on_device,
        mesh=mesh,
        in_specs=(
            P(("groups", "tx"), None),
            P(("groups", "tx"), None),
            P(("groups", "tx"), None),
            P(("groups", "tx")),
            P(("groups", "tx")),
            P(("groups", "tx")),
            P(),
            P(),
            P(),
            P(("groups", "tx"), None),
        ),
        out_specs=(P(("groups", "tx"), None), P(("groups", "tx"), None), P(("groups", "tx"), None)),
        check_vma=False,
    )
```

time: 258 us -> 171 us (0.66)
  matrix products: 87.7 us -> 8.42 us
  waiting for transfers between devices: 26.3 us -> 88.4 us
  other arithmetic: 62.5 us -> 3.74 us
  local copies, waits for them, and re-layouts: 46.4 us -> 3.9 us
  blocking collectives: 0 us -> 23.3 us
  starting transfers between devices: 31 us -> 11.7 us
  Pallas kernels: 0 us -> 16.2 us
  between operations: 0.9 us -> 14.9 us
    unnamed x0 -> x2, waiting for transfers between devices: none -> 87.1 us
    dot_general x30 -> x2, matrix products: 80.8 us -> 1.46 us  [the longest x1 1.19 us: on_device(): jnp.dot(chosen.astype(jnp.float32).T, grad_patch, precision=lax.Precision...]
    another operation x2 -> x0, other arithmetic: 47.6 us -> none  [all_column_bands(): jnp.stack([from_real, from_imag], axis=2)]
    another operation x1 -> x0, local copies, waits for them, and re-layouts: 28.4 us -> none  [all_column_bands(): jnp.stack([from_real, from_imag], axis=2)]
    all_gather x0 -> x1, blocking collectives: none -> 23.3 us  [on_device(): lax.all_gather(masters.astype(jnp.bfloat16), 'tx', axis=0, tiled=True)]
    all_to_all x3 -> x0, waiting for transfers between devices: 23.1 us -> none  [the longest x1 23.1 us: on_device(): lax.all_to_all(slot_grads, 'tx', split_axis=0, concat_axis=0, tiled=True)]
    all_to_all x3 -> x0, starting transfers between devices: 19.8 us -> none  [the longest x1 7.35 us: on_device(): lax.all_to_all(requests, 'tx', split_axis=0, concat_axis=0, tiled=True)]
    pallas_call x0 -> x1, Pallas kernels: none -> 16.2 us  [run_filters(): pl.pallas_call(body, out_shape=(jax.ShapeDtypeStruct((rows_here, W), jnp....]
  transfers between devices with their start and end apart: 7 -> 5, of which waited for: 2 -> 3; matrix products, arithmetic and copies ran while one was open for 42% -> 1% of each run, Pallas kernels for 0% -> 0%
where the time goes in v1:
time: 171 us
  waiting for transfers between devices  88.4 us (52%)
  blocking collectives  23.3 us (14%)
  Pallas kernels  16.2 us (9%)
  between operations  14.9 us (9%)
  starting transfers between devices  11.7 us (7%)
  matrix products  8.42 us (5%)
  local copies, waits for them, and re-layouts  3.9 us (2%)
  other arithmetic  3.74 us (2%)
    unnamed x2, waiting for transfers between devices  87.1 us
    all_gather x1, blocking collectives, on_device(): lax.all_gather(masters.astype(jnp.bfloat16), 'tx', axis=0, tiled=True)  23.3 us
    pallas_call x1, Pallas kernels, run_filters(): pl.pallas_call(body, out_shape=(jax.ShapeDtypeStruct((rows_here, W), jnp....  16.2 us
    ppermute x1, starting transfers between devices, on_device(): lax.ppermute(grad_padded[HALF + rows_here:2 * HALF + rows_here], 'tx', [(...  4.2 us
    ppermute x1, starting transfers between devices, halo(): low = lax.ppermute(block[-width:], axis, forward)  3.49 us
  transfers between devices with their start and end apart: 5, of which 3 were waited for; matrix products, arithmetic and copies ran while one was open for 1% of the time, Pallas kernels for 0%

profile of v1, /device:TPU:1, one launch (start us, length us, event | category | flops | bytes accessed | tf_op | source)
XLA Modules:
  0.0 170.6 jit_solution(416147221771622879)
XLA Ops:
  7.3 0.7 convert_bitcast_fusion
  8.0 23.3 %all-gather = bf16[16,4,1024]{2,1,0:T(4,128)(2,1)S(1)} all-gather(bf16[1,4,1024]{2,1,0:T(4,128)(2,1)S(1)} %convert_bitcast_fusion), channel_id=1, replica_groups=mesh['groups'=2,'tx'=16] {'tx'}, dimensions={0}, use_global_device_ids=true | all-gather | bytes 139264 | tf_op jit(solution)/shard_map/all_gather | solution.py:207
  31.3 0.7 bitcast_add_fusion
  32.0 0.3 convolution_convert_fusion
  32.3 0.2 copy.15
  32.5 1.4 copy.16
  33.9 0.8 iota_add_fusion
  34.7 1.9 %fusion.11 = bf16[64,256]{1,0:T(8,128)(2,1)S(1)} fusion(bf16[128,32,32]{2,1,0:T(8,128)(2,1)S(1)} %copy.16, s32[128,32]{1,0:T(8,128)S(1)} %get-tuple-element.13, s32[128,32]{1,0:T(8,128)S(1)} %get-tuple-element.14), kind=kOutput, calls=%fused_computation.11 | convolution fusion | flops 203702272 | bytes 327680 | tf_op jit(solution)/shard_map/pai,paj->ij/dot_general | solution.py:232
  36.6 2.1 %collective-permute-start.1 = (bf16[31,256]{1,0:T(8,128)(2,1)S(1)}, bf16[31,256]{1,0:T(8,128)(2,1)S(1)}, u32[]{:S(2)}, u32[]{:S(2)}) collective-permute-start(bf16[31,256]{1,0:T(8,128)(2,1)S(1)} %get-tuple-element.12), channel_id=1, source_target_pairs={{1,0},{2,1},{3,2},{4,3},{5,4},{6,5},{7,6},{8,7},{9,8},{10,9},{11,1... | collective-permute-start | bytes 47624 | tf_op jit(solution)/shard_map/ppermute | solution.py:29
  38.7 3.5 %collective-permute-start = (bf16[31,256]{1,0:T(8,128)(2,1)S(1)}, bf16[31,256]{1,0:T(8,128)(2,1)S(1)}, u32[]{:S(2)}, u32[]{:S(2)}) collective-permute-start(bf16[31,256]{1,0:T(8,128)(2,1)S(1)} %get-tuple-element.11), channel_id=1, source_target_pairs={{0,1},{1,2},{2,3},{3,4},{4,5},{5,6},{6,7},{7,8},{8,9},{9,10},{10,1... | collective-permute-start | bytes 47624 | tf_op jit(solution)/shard_map/ppermute | solution.py:28
  42.4 0.1 select_maximum_fusion.refs_2_
  42.8 0.3 collective-permute-done
  43.1 0.1 fusion.23.refs_5_
  43.2 16.2 %filters.1 = (f32[64,256]{1,0:T(8,128)}, f32[128,256]{1,0:T(8,128)S(1)}) custom-call(f32[12]{0:T(128)S(1)} %copy-done.1, f32[12,8,128]{2,1,0:T(8,128)S(1)} %pad.27.refs_1_, f32[12,8,128]{2,1,0:T(8,128)S(1)} %select_maximum_fusion.refs_2_, f32[12,8,128]{2,1,0:T(8,128)S(1)} %pad.29.refs_3_, f32[12,8,128]{2,1,0:T(8,128)S(1)} %pad.30.refs_4_, ...), custom_call_target="tpu_custom_call" | custom-call | tf_op jit(solution)/shard_map/filters/pallas_call | solution.py:177
  59.4 1.9 %collective-permute-start.3 = (f32[31,256]{1,0:T(8,128)S(1)}, f32[31,256]{1,0:T(8,128)S(1)}, u32[]{:S(2)}, u32[]{:S(2)}) collective-permute-start(f32[31,256]{1,0:T(8,128)S(1)} %get-tuple-element.10), channel_id=1, source_target_pairs={{1,0},{2,1},{3,2},{4,3},{5,4},{6,5},{7,6},{8,7},{9,8},{10,9},{11,1... | collective-permute-start | bytes 95240 | tf_op jit(solution)/shard_map/ppermute | solution.py:246
  61.3 4.2 %collective-permute-start.2 = (f32[31,256]{1,0:T(8,128)S(1)}, f32[31,256]{1,0:T(8,128)S(1)}, u32[]{:S(2)}, u32[]{:S(2)}) collective-permute-start(f32[31,256]{1,0:T(8,128)S(1)} %get-tuple-element.9), channel_id=1, source_target_pairs={{0,1},{1,2},{2,3},{3,4},{4,5},{5,6},{6,7},{7,8},{8,9},{9,10},{10,1... | collective-permute-start | bytes 95240 | tf_op jit(solution)/shard_map/ppermute | solution.py:241
  65.6 1.0 collective-permute-done.2
  66.6 1.9 %fusion.7 = f32[128,32,256]{2,1,0:T(8,128)S(1)} fusion(s32[128,32]{1,0:T(8,128)S(1)} %get-tuple-element.14, f32[31,256]{1,0:T(8,128)S(1)} %collective-permute-done.3, f32[31,256]{1,0:T(8,128)S(1)} %collective-permute-done.2, f32[128,256]{1,0:T(8,128)S(1)} %get-tuple-element.6), kind=kOutput, calls=%fused_computation.8 | convolution fusion | flops 805601280 | bytes 4390912 | tf_op jit(solution)/shard_map/pai,ij->paj/dot_general | solution.py:250
  68.5 3.1 %fusion = f32[128,32,32]{2,1,0:T(8,128)S(1)} fusion(f32[128,32,256]{2,1,0:T(8,128)S(1)} %fusion.7, s32[128,32]{1,0:T(8,128)S(1)} %get-tuple-element.13), kind=kOutput, calls=%fused_computation.1 | convolution fusion | flops 403701760 | bytes 4734976 | tf_op jit(solution)/shard_map/paj,pcj->pac/dot_general | solution.py:253
  71.6 1.2 copy.19
  72.9 1.2 fusion.33
  74.1 0.6 dynamic-slice
  75.3 87.0 %all-reduce.10.cloned.1.call-done = f32[64,1024]{1,0:T(8,128)} async-done(((f32[64,1024]{1,0:T(8,128)}), f32[64,1024]{1,0:T(8,128)}) %all-reduce.10.cloned.1.call-update) | async-done | bytes 262160
  162.4 1.4 multiply_subtract_fusion
  (28 shorter events, 0.6 us)
Async XLA Ops:
  7.2 35.0 %copy-start.2 = (bf16[12,4,2,63]{3,2,1,0:T(2,128)(2,1)S(1)}, bf16[12,4,2,63]{3,2,1,0:T(2,128)(2,1)}, u32[]{:S(2)}) copy-start(bf16[12,4,2,63]{3,2,1,0:T(2,128)(2,1)} %param.16) | copy-start | bytes 36292
  7.2 35.3 %copy-start.3 = (bf16[12,4,2,63]{3,2,1,0:T(2,128)(2,1)S(1)}, bf16[12,4,2,63]{3,2,1,0:T(2,128)(2,1)}, u32[]{:S(2)}) copy-start(bf16[12,4,2,63]{3,2,1,0:T(2,128)(2,1)} %param.17) | copy-start | bytes 36292
  7.2 36.0 %copy-start.1 = (f32[12]{0:T(128)S(1)}, f32[12]{0:T(128)}, u32[]{:S(2)}) copy-start(f32[12]{0:T(128)} %refs_0_.1) | copy-start | bytes 148
  7.2 36.0 %copy-start = (bf16[64,256]{1,0:T(8,128)(2,1)S(1)}, bf16[64,256]{1,0:T(8,128)(2,1)}, u32[]{:S(2)}) copy-start(bf16[64,256]{1,0:T(8,128)(2,1)} %refs_6_.1) | copy-start | bytes 98308
  7.2 155.2 %all-reduce.10.cloned.1.call-start = ((), (), s32[]{:S(2)}) async-start(), calls=%async_computation | async-start | bytes 524288
  36.6 6.1 %collective-permute-start.1 = (bf16[31,256]{1,0:T(8,128)(2,1)S(1)}, bf16[31,256]{1,0:T(8,128)(2,1)S(1)}, u32[]{:S(2)}, u32[]{:S(2)}) collective-permute-start(bf16[31,256]{1,0:T(8,128)(2,1)S(1)} %get-tuple-element.12), channel_id=1, source_target_pairs={{1,0},{2,1},{3,2},{4,3},{5,4},{6,5},{7,6},{8,7},{9,8},{10,9},{11,1... | collective-permute-start | bytes 47624 | tf_op jit(solution)/shard_map/ppermute | solution.py:29
  38.7 4.3 %collective-permute-start = (bf16[31,256]{1,0:T(8,128)(2,1)S(1)}, bf16[31,256]{1,0:T(8,128)(2,1)S(1)}, u32[]{:S(2)}, u32[]{:S(2)}) collective-permute-start(bf16[31,256]{1,0:T(8,128)(2,1)S(1)} %get-tuple-element.11), channel_id=1, source_target_pairs={{0,1},{1,2},{2,3},{3,4},{4,5},{5,6},{6,7},{7,8},{8,9},{9,10},{10,1... | collective-permute-start | bytes 47624 | tf_op jit(solution)/shard_map/ppermute | solution.py:28
  59.4 6.1 %collective-permute-start.3 = (f32[31,256]{1,0:T(8,128)S(1)}, f32[31,256]{1,0:T(8,128)S(1)}, u32[]{:S(2)}, u32[]{:S(2)}) collective-permute-start(f32[31,256]{1,0:T(8,128)S(1)} %get-tuple-element.10), channel_id=1, source_target_pairs={{1,0},{2,1},{3,2},{4,3},{5,4},{6,5},{7,6},{8,7},{9,8},{10,9},{11,1... | collective-permute-start | bytes 95240 | tf_op jit(solution)/shard_map/ppermute | solution.py:246
  61.3 5.2 %collective-permute-start.2 = (f32[31,256]{1,0:T(8,128)S(1)}, f32[31,256]{1,0:T(8,128)S(1)}, u32[]{:S(2)}, u32[]{:S(2)}) collective-permute-start(f32[31,256]{1,0:T(8,128)S(1)} %get-tuple-element.9), channel_id=1, source_target_pairs={{0,1},{1,2},{2,3},{3,4},{4,5},{5,6},{6,7},{7,8},{8,9},{9,10},{10,1... | collective-permute-start | bytes 95240 | tf_op jit(solution)/shard_map/ppermute | solution.py:241
  68.5 5.6 %copy-start.6 = (u32[32]{0:T(128)S(1)}, u32[32]{0:T(128)}, u32[]{:S(2)}) copy-start(u32[32]{0:T(128)} %constant.29) | copy-start | bytes 388
  68.5 93.9 %copy-start.4 = (f32[4,1024]{1,0:T(4,128)S(1)}, f32[4,1024]{1,0:T(4,128)}, u32[]{:S(2)}) copy-start(f32[4,1024]{1,0:T(4,128)} %param.10) | copy-start | bytes 49156
  68.5 93.9 %copy-start.5 = (f32[4,1024]{1,0:T(4,128)S(1)}, f32[4,1024]{1,0:T(4,128)}, u32[]{:S(2)}) copy-start(f32[4,1024]{1,0:T(4,128)} %param.11) | copy-start | bytes 49156
Sparse Core Ops, SparseCore 0:
  74.2 88.1 all-reduce.9

commit v2 on v1

--- a/solution.py
+++ b/solution.py
@@ -28,6 +28,80 @@
     low = lax.ppermute(block[-width:], axis, forward)
     high = lax.ppermute(block[:width], axis, backward)
     return low, high
+
+
+def exchange(n, source, slots, send_sem, recv_sem):
+    me = lax.axis_index("tx")
+    barrier = pltpu.get_barrier_semaphore()
+
+    def greet(step, carry):
+        peer = lax.rem(me + step, n)
+        pl.semaphore_signal(
+            barrier, inc=1, device_id={"tx": peer}, device_id_type=pl.DeviceIdType.MESH
+        )
+        return carry
+
+    lax.fori_loop(1, n, greet, 0)
+    pl.semaphore_wait(barrier, n - 1)
+
+    def copy(step):
+        peer = lax.rem(me + step, n)
+        return pltpu.make_async_remote_copy(
+            src_ref=source(peer),
+            dst_ref=slots.at[step],
+            send_sem=send_sem.at[step],
+            recv_sem=recv_sem.at[step],
+            device_id={"tx": peer},
+            device_id_type=pl.DeviceIdType.MESH,
+        )
+
+    def start(step, carry):
+        copy(step).start()
+        return carry
+
+    def finish(step, carry):
+        copy(step).wait()
+        return carry
+
+    lax.fori_loop(1, n, start, 0)
+    return me, lambda: lax.fori_loop(1, n, finish, 0)
+
+
+def gather_kernel(n, block_ref, out_ref, slots, send_sem, recv_sem):
+    _, finish = exchange(n, lambda peer: block_ref, slots, send_sem, recv_sem)
+    out_ref[0] = block_ref[...]
+    finish()
+    out_ref[1:] = slots[1:]
+
+
+def scatter_sum_kernel(n, parts_ref, out_ref, slots, send_sem, recv_sem):
+    me, finish = exchange(n, lambda peer: parts_ref.at[peer], slots, send_sem, recv_sem)
+    own = parts_ref[me]
+    finish()
+    out_ref[...] = own + jnp.sum(slots[1:], axis=0)
+
+
+def exchange_call(kernel, n, value, out_shape, collective_id, name):
+    vmem = pl.BlockSpec(memory_space=pltpu.VMEM)
+
+    def body(*refs):
+        kernel(n, *refs)
+
+    return pl.pallas_call(
+        body,
+        out_shape=jax.ShapeDtypeStruct(out_shape, value.dtype),
+        in_specs=[vmem],
+        out_specs=vmem,
+        scratch_shapes=[
+            pltpu.VMEM((n,) + value.shape[-2:], value.dtype),
+            pltpu.SemaphoreType.DMA((n,)),
+            pltpu.SemaphoreType.DMA((n,)),
+        ],
+        compiler_params=pltpu.CompilerParams(
+            collective_id=collective_id, has_side_effects=True, vmem_limit_bytes=24 * 1024 * 1024
+        ),
+        name=name,
+    )(value)
 
 
 def tap_rows(row_taps, col_taps):
@@ -204,8 +278,18 @@
     places = place_local.shape[0]
     devices = lax.axis_size("tx")
     master_count = masters.shape[0]
-    all_masters = lax.all_gather(masters.astype(jnp.bfloat16), "tx", axis=0, tiled=True)
+    tiles = master_count * MS * MS // LANES
+    all_masters = exchange_call(
+        gather_kernel,
+        devices,
+        masters.astype(jnp.bfloat16).reshape(tiles, LANES),
+        (devices, tiles, LANES),
+        0,
+        "gather_masters",
+    ).reshape(devices * master_count, MS * MS)
     master_id = place_owner[:, 0] * master_count + place_local
+    distance = lax.rem(lax.axis_index("tx") - place_owner[:, 0] + devices, devices)
+    slot_id = distance * master_count + place_local
     offsets = jnp.arange(MS, dtype=jnp.int32)
     row_chosen = (
         place_row[:, None, None] + offsets[None, :, None]
@@ -215,11 +299,11 @@
         place_col[:, None, None] + offsets[None, :, None]
         == jnp.arange(W, dtype=jnp.int32)[None, None, :]
     )
-    chosen = (
-        master_id[:, None] == jnp.arange(devices * master_count, dtype=jnp.int32)[None, :]
-    )
+    master_iota = jnp.arange(devices * master_count, dtype=jnp.int32)[None, :]
+    chosen = master_id[:, None] == master_iota
+    slot_chosen = slot_id[:, None] == master_iota
     pattern_half = (
-        jnp.dot(chosen.astype(jnp.bfloat16), all_masters, preferred_element_type=jnp.float32)
+        jnp.dot(slot_chosen.astype(jnp.bfloat16), all_masters, preferred_element_type=jnp.float32)
         .astype(jnp.bfloat16)
         .reshape(places, MS, MS)
     )
@@ -256,7 +340,14 @@
     partial = jnp.dot(
         chosen.astype(jnp.float32).T, grad_patch, precision=lax.Precision.HIGHEST
     )
-    master_grad = lax.psum_scatter(partial, "tx", scatter_dimension=0, tiled=True)
+    master_grad = exchange_call(
+        scatter_sum_kernel,
+        devices,
+        partial.reshape(devices, tiles, LANES),
+        (tiles, LANES),
+        1,
+        "sum_gradients",
+    ).reshape(master_count, MS * MS)
     velocity_new = momentum * velocity + master_grad
     masters_new = masters - step_size * velocity_new
     return (resist_residual, velocity_new, masters_new)

time: 171 us -> 69.4 us (0.41)
  waiting for transfers between devices: 88.4 us -> 3.54 us
  blocking collectives: 23.3 us -> 0 us
  Pallas kernels: 16.2 us -> 35.9 us
  between operations: 14.9 us -> 0.92 us
    unnamed x2 -> x0, waiting for transfers between devices: 87.1 us -> none
    all_gather x1 -> x0, blocking collectives: 23.3 us -> none  [on_device(): lax.all_gather(masters.astype(jnp.bfloat16), 'tx', axis=0, tiled=True)]
    pallas_call x0 -> x2, Pallas kernels: none -> 19.7 us  [exchange_call(): pl.pallas_call(body, out_shape=jax.ShapeDtypeStruct(out_shape, value.dtyp...]
    ppermute x1, waiting for transfers between devices: 0.01 us -> 2.59 us  [halo(): high = lax.ppermute(block[:width], axis, backward)]
    ppermute x1, starting transfers between devices: 4.2 us -> 1.93 us  [on_device(): lax.ppermute(grad_padded[HALF + rows_here:2 * HALF + rows_here], 'tx', [(...]
  transfers between devices with their start and end apart: 5 -> 4, of which waited for: 3 -> 2; matrix products, arithmetic and copies ran while one was open for 1% -> 3% of each run, Pallas kernels for 0% -> 0%
where the time goes in v2:
time: 69.4 us; the launch traced here: 69 us
  Pallas kernels  35.9 us (52%)
  starting transfers between devices  10.3 us (15%)
  matrix products  9.43 us (14%)
  local copies, waits for them, and re-layouts  5.15 us (7%)
  other arithmetic  3.76 us (5%)
  waiting for transfers between devices  3.54 us (5%)
  between operations  0.92 us (1%)
    pallas_call x2, Pallas kernels, exchange_call(): pl.pallas_call(body, out_shape=jax.ShapeDtypeStruct(out_shape, value.dtyp...  19.7 us
    pallas_call x1, Pallas kernels, run_filters(): pl.pallas_call(body, out_shape=(jax.ShapeDtypeStruct((rows_here, W), jnp....  16.2 us
    ppermute x1, starting transfers between devices, halo(): low = lax.ppermute(block[-width:], axis, forward)  3.84 us
    dot_general x1, matrix products, on_device(): jnp.einsum('paj,pcj->pac', row_rows, col_chosen.astype(jnp.float32), prec...  3.12 us
    ppermute x1, waiting for transfers between devices, halo(): high = lax.ppermute(block[:width], axis, backward)  2.59 us
    ppermute x1, starting transfers between devices, on_device(): lax.ppermute(grad_padded[:HALF], 'tx', [(i + 1, i) for i in range(count -...  2.57 us
    dot_general x1, matrix products, on_device(): jnp.einsum('pai,paj->ij', row_chosen.astype(jnp.bfloat16), spread, prefer...  2.38 us
    ppermute x1, starting transfers between devices, on_device(): lax.ppermute(grad_padded[HALF + rows_here:2 * HALF + rows_here], 'tx', [(...  1.93 us
  transfers between devices with their start and end apart: 4, of which 2 were waited for; matrix products, arithmetic and copies ran while one was open for 3% of the time, Pallas kernels for 0%

profile of v2, /device:TPU:1, one launch (start us, length us, event | category | flops | bytes accessed | tf_op | source)
XLA Modules:
  0.0 69.0 jit_solution(14601483254833366708)
XLA Ops:
  0.6 0.7 %convert_element_type.47 = bf16[4,1024]{1,0:T(4,128)(2,1)S(1)} convert(f32[4,1024]{1,0:T(4,128)} %param.10) | non-fusion elementwise | flops 4096 | bytes 24576 | tf_op jit(solution)/shard_map/convert_element_type | solution.py:285
  1.4 0.7 iota_add_fusion.1
  2.0 0.7 %iota_add_fusion = s32[128,32]{1,0:T(8,128)S(1)} fusion(s32[128]{0:T(128)} %param.15), kind=kLoop, calls=%fused_computation.32 | loop fusion | flops 4096 | bytes 16896 | tf_op jit(solution)/shard_map/add | solution.py:299
  2.8 9.4 %gather_masters.1 = bf16[16,32,128]{2,1,0:T(8,128)(2,1)S(1)} custom-call(bf16[32,128]{1,0:T(8,128)(2,1)S(1)} %reshape.88.refs_0_), custom_call_target="tpu_custom_call" | custom-call | tf_op jit(solution)/shard_map/gather_masters/pallas_call | solution.py:90
  12.2 0.7 bitcast_add_fusion
  12.9 0.3 convolution_convert_fusion
  13.2 0.2 copy.13
  13.4 1.4 %copy.15 = bf16[128,32,32]{2,1,0:T(8,128)(2,1)S(1)} copy(bf16[128,32,32]{0,2,1:T(8,128)(2,1)S(1)} %bitcast.23) | data formatting | bytes 524288 | tf_op jit(solution)/shard_map/reshape | solution.py:308
  14.8 1.3 %fusion.1 = bf16[128,32,256]{2,1,0:T(8,128)(2,1)S(1)} fusion(bf16[128,32,32]{2,1,0:T(8,128)(2,1)S(1)} %copy.15, s32[128,32]{1,0:T(8,128)S(1)} %iota_add_fusion), kind=kOutput, calls=%fused_computation.3 | convolution fusion | flops 68157440 | bytes 2375680 | tf_op jit(solution)/shard_map/pab,pbj->paj/dot_general | solution.py:310
  16.2 2.4 %fusion.6 = bf16[64,256]{1,0:T(8,128)(2,1)S(1)} fusion(bf16[128,32,256]{2,1,0:T(8,128)(2,1)S(1)} %fusion.1, s32[128,32]{0,1:T(8,128)S(1)} %iota_add_fusion.1), kind=kOutput, calls=%fused_computation.9 | convolution fusion | flops 134496256 | bytes 2146304 | tf_op jit(solution)/shard_map/pai,paj->ij/dot_general | solution.py:316
  18.6 3.8 %collective-permute-start = (bf16[31,256]{1,0:T(8,128)(2,1)S(1)}, bf16[31,256]{1,0:T(8,128)(2,1)S(1)}, u32[]{:S(2)}, u32[]{:S(2)}) collective-permute-start(bf16[31,256]{1,0:T(8,128)(2,1)S(1)} %get-tuple-element.11), channel_id=1, source_target_pairs={{0,1},{1,2},{2,3},{3,4},{4,5},{5,6},{6,7},{7,8},{8,9},{9,10},{10,1... | collective-permute-start | bytes 47624 | tf_op jit(solution)/shard_map/ppermute | solution.py:28
  22.4 1.9 %collective-permute-start.1 = (bf16[31,256]{1,0:T(8,128)(2,1)S(1)}, bf16[31,256]{1,0:T(8,128)(2,1)S(1)}, u32[]{:S(2)}, u32[]{:S(2)}) collective-permute-start(bf16[31,256]{1,0:T(8,128)(2,1)S(1)} %get-tuple-element.12), channel_id=1, source_target_pairs={{1,0},{2,1},{3,2},{4,3},{5,4},{6,5},{7,6},{8,7},{9,8},{10,9},{11,1... | collective-permute-start | bytes 47624 | tf_op jit(solution)/shard_map/ppermute | solution.py:29
  24.9 2.6 %collective-permute-done.1 = bf16[31,256]{1,0:T(8,128)(2,1)S(1)} collective-permute-done((bf16[31,256]{1,0:T(8,128)(2,1)S(1)}, bf16[31,256]{1,0:T(8,128)(2,1)S(1)}, u32[]{:S(2)}, u32[]{:S(2)}) %collective-permute-start.1) | collective-permute-done | bytes 15904 | tf_op jit(solution)/shard_map/ppermute | solution.py:29
  27.6 16.2 %filters.1 = (f32[64,256]{1,0:T(8,128)}, f32[128,256]{1,0:T(8,128)S(1)}) custom-call(f32[12]{0:T(128)S(1)} %copy-done.1, f32[12,8,128]{2,1,0:T(8,128)S(1)} %pad.27.refs_1_, f32[12,8,128]{2,1,0:T(8,128)S(1)} %select_maximum_fusion.refs_2_, f32[12,8,128]{2,1,0:T(8,128)S(1)} %pad.29.refs_3_, f32[12,8,128]{2,1,0:T(8,128)S(1)} %pad.30.refs_4_, ...), custom_call_target="tpu_custom_call" | custom-call | tf_op jit(solution)/shard_map/filters/pallas_call | solution.py:251
  43.8 1.9 %collective-permute-start.2 = (f32[31,256]{1,0:T(8,128)S(1)}, f32[31,256]{1,0:T(8,128)S(1)}, u32[]{:S(2)}, u32[]{:S(2)}) collective-permute-start(f32[31,256]{1,0:T(8,128)S(1)} %get-tuple-element.9), channel_id=1, source_target_pairs={{0,1},{1,2},{2,3},{3,4},{4,5},{5,6},{6,7},{7,8},{8,9},{9,10},{10,1... | collective-permute-start | bytes 95240 | tf_op jit(solution)/shard_map/ppermute | solution.py:325
  45.8 2.6 %collective-permute-start.3 = (f32[31,256]{1,0:T(8,128)S(1)}, f32[31,256]{1,0:T(8,128)S(1)}, u32[]{:S(2)}, u32[]{:S(2)}) collective-permute-start(f32[31,256]{1,0:T(8,128)S(1)} %get-tuple-element.10), channel_id=1, source_target_pairs={{1,0},{2,1},{3,2},{4,3},{5,4},{6,5},{7,6},{8,7},{9,8},{10,9},{11,1... | collective-permute-start | bytes 95240 | tf_op jit(solution)/shard_map/ppermute | solution.py:330
  48.5 1.7 %copy.17 = pred[128,32,64]{2,1,0:T(32,128)(4,1)S(1)} copy(pred[128,32,64]{0,2,1:T(32,128)(4,1)S(1)} %iota_compare_fusion.3) | data formatting | bytes 524288 | tf_op jit(solution)/shard_map/eq | solution.py:295
  50.2 0.9 %collective-permute-done.3 = f32[31,256]{1,0:T(8,128)S(1)} collective-permute-done((f32[31,256]{1,0:T(8,128)S(1)}, f32[31,256]{1,0:T(8,128)S(1)}, u32[]{:S(2)}, u32[]{:S(2)}) %collective-permute-start.3) | collective-permute-done | bytes 31776 | tf_op jit(solution)/shard_map/ppermute | solution.py:330
  51.1 1.8 %fusion.17 = f32[128,32,256]{2,1,0:T(8,128)S(1)} fusion(pred[128,32,64]{2,1,0:T(32,128)(4,1)S(1)} %copy.17, f32[31,256]{1,0:T(8,128)S(1)} %collective-permute-done.3, f32[31,256]{1,0:T(8,128)S(1)} %collective-permute-done.2, f32[128,256]{1,0:T(8,128)S(1)} %get-tuple-element.6), kind=kOutput, calls=%fused_computation.24 | convolution fusion | flops 805339136 | bytes 4849664 | tf_op jit(solution)/shard_map/pai,ij->paj/dot_general | solution.py:334
  53.0 3.1 %fusion = f32[128,32,32]{2,1,0:T(8,128)S(1)} fusion(f32[128,32,256]{2,1,0:T(8,128)S(1)} %fusion.17, s32[128,32]{1,0:T(8,128)S(1)} %iota_add_fusion), kind=kOutput, calls=%fused_computation.2 | convolution fusion | flops 403701760 | bytes 4734976 | tf_op jit(solution)/shard_map/paj,pcj->pac/dot_general | solution.py:337
  56.1 1.3 %copy.14 = f32[128,32,32]{0,2,1:T(8,128)S(1)} copy(f32[128,32,32]{2,1,0:T(8,128)S(1)} %fusion) | data formatting | bytes 1048576 | tf_op jit(solution)/shard_map/paj,pcj->pac/dot_general | solution.py:337
  57.4 0.5 fusion.25
  58.0 10.4 %sum_gradients.1 = f32[32,128]{1,0:T(8,128)S(1)} custom-call(f32[16,32,128]{2,1,0:T(8,128)S(1)} %reshape.92.refs_0_), custom_call_target="tpu_custom_call" | custom-call | tf_op jit(solution)/shard_map/sum_gradients/pallas_call | solution.py:90
  68.4 0.6 multiply_subtract_fusion
  (30 shorter events, 0.9 us)
Async XLA Ops:
  12.1 12.2 %copy-start.2 = (bf16[12,4,2,63]{3,2,1,0:T(2,128)(2,1)S(1)}, bf16[12,4,2,63]{3,2,1,0:T(2,128)(2,1)}, u32[]{:S(2)}) copy-start(bf16[12,4,2,63]{3,2,1,0:T(2,128)(2,1)} %param.16) | copy-start | bytes 36292
  13.2 11.4 %copy-start.3 = (bf16[12,4,2,63]{3,2,1,0:T(2,128)(2,1)S(1)}, bf16[12,4,2,63]{3,2,1,0:T(2,128)(2,1)}, u32[]{:S(2)}) copy-start(bf16[12,4,2,63]{3,2,1,0:T(2,128)(2,1)} %param.17) | copy-start | bytes 36292
  13.4 14.2 %copy-start = (bf16[64,256]{1,0:T(8,128)(2,1)S(1)}, bf16[64,256]{1,0:T(8,128)(2,1)}, u32[]{:S(2)}) copy-start(bf16[64,256]{1,0:T(8,128)(2,1)} %refs_6_.1) | copy-start | bytes 98308
  13.4 14.2 %copy-start.1 = (f32[12]{0:T(128)S(1)}, f32[12]{0:T(128)}, u32[]{:S(2)}) copy-start(f32[12]{0:T(128)} %refs_0_.1) | copy-start | bytes 148
  18.6 6.3 %collective-permute-start = (bf16[31,256]{1,0:T(8,128)(2,1)S(1)}, bf16[31,256]{1,0:T(8,128)(2,1)S(1)}, u32[]{:S(2)}, u32[]{:S(2)}) collective-permute-start(bf16[31,256]{1,0:T(8,128)(2,1)S(1)} %get-tuple-element.11), channel_id=1, source_target_pairs={{0,1},{1,2},{2,3},{3,4},{4,5},{5,6},{6,7},{7,8},{8,9},{9,10},{10,1... | collective-permute-start | bytes 47624 | tf_op jit(solution)/shard_map/ppermute | solution.py:28
  22.4 5.1 %collective-permute-start.1 = (bf16[31,256]{1,0:T(8,128)(2,1)S(1)}, bf16[31,256]{1,0:T(8,128)(2,1)S(1)}, u32[]{:S(2)}, u32[]{:S(2)}) collective-permute-start(bf16[31,256]{1,0:T(8,128)(2,1)S(1)} %get-tuple-element.12), channel_id=1, source_target_pairs={{1,0},{2,1},{3,2},{4,3},{5,4},{6,5},{7,6},{8,7},{9,8},{10,9},{11,1... | collective-permute-start | bytes 47624 | tf_op jit(solution)/shard_map/ppermute | solution.py:29
  43.8 6.4 %collective-permute-start.2 = (f32[31,256]{1,0:T(8,128)S(1)}, f32[31,256]{1,0:T(8,128)S(1)}, u32[]{:S(2)}, u32[]{:S(2)}) collective-permute-start(f32[31,256]{1,0:T(8,128)S(1)} %get-tuple-element.9), channel_id=1, source_target_pairs={{0,1},{1,2},{2,3},{3,4},{4,5},{5,6},{6,7},{7,8},{8,9},{9,10},{10,1... | collective-permute-start | bytes 95240 | tf_op jit(solution)/shard_map/ppermute | solution.py:325
  45.8 5.4 %collective-permute-start.3 = (f32[31,256]{1,0:T(8,128)S(1)}, f32[31,256]{1,0:T(8,128)S(1)}, u32[]{:S(2)}, u32[]{:S(2)}) collective-permute-start(f32[31,256]{1,0:T(8,128)S(1)} %get-tuple-element.10), channel_id=1, source_target_pairs={{1,0},{2,1},{3,2},{4,3},{5,4},{6,5},{7,6},{8,7},{9,8},{10,9},{11,1... | collective-permute-start | bytes 95240 | tf_op jit(solution)/shard_map/ppermute | solution.py:330
  53.0 15.4 %copy-start.4 = (f32[4,1024]{1,0:T(4,128)S(1)}, f32[4,1024]{1,0:T(4,128)}, u32[]{:S(2)}) copy-start(f32[4,1024]{1,0:T(4,128)} %param.10) | copy-start | bytes 49156
  53.0 15.4 %copy-start.5 = (f32[4,1024]{1,0:T(4,128)S(1)}, f32[4,1024]{1,0:T(4,128)}, u32[]{:S(2)}) copy-start(f32[4,1024]{1,0:T(4,128)} %param.11) | copy-start | bytes 49156

commit v3 on v2

--- a/solution.py
+++ b/solution.py
@@ -21,13 +21,70 @@
 step_size = 0.05
 
 
-def halo(block, axis, width):
-    count = lax.axis_size(axis)
-    forward = [(i, i + 1) for i in range(count - 1)]
-    backward = [(target, source) for source, target in forward]
-    low = lax.ppermute(block[-width:], axis, forward)
-    high = lax.ppermute(block[:width], axis, backward)
+def swap_rims(first, second, slots, send_sem, recv_sem):
+    n = lax.axis_size("tx")
+    me = lax.axis_index("tx")
+    before, after = lax.rem(me + n - 1, n), lax.rem(me + 1, n)
+    barrier = pltpu.get_barrier_semaphore()
+    for peer in (before, after):
+        pl.semaphore_signal(
+            barrier, inc=1, device_id={"tx": peer}, device_id_type=pl.DeviceIdType.MESH
+        )
+    pl.semaphore_wait(barrier, 2)
+    copies = [
+        pltpu.make_async_remote_copy(
+            src_ref=source,
+            dst_ref=slots.at[slot],
+            send_sem=send_sem.at[slot],
+            recv_sem=recv_sem.at[slot],
+            device_id={"tx": peer},
+            device_id_type=pl.DeviceIdType.MESH,
+        )
+        for source, slot, peer in ((first, 1, before), (second, 0, after))
+    ]
+    for copy in copies:
+        copy.start()
+    for copy in copies:
+        copy.wait()
+    low = jnp.where(me > 0, slots[0].astype(jnp.float32), 0.0)
+    high = jnp.where(me < n - 1, slots[1].astype(jnp.float32), 0.0)
     return low, high
+
+
+def mask_rims_kernel(mask_ref, out_ref, slots, send_sem, recv_sem):
+    rows, rim = mask_ref.shape[0], slots.shape[1]
+    low, high = swap_rims(
+        mask_ref.at[pl.ds(0, rim)], mask_ref.at[pl.ds(rows - rim, rim)], slots, send_sem, recv_sem
+    )
+    out_ref[:rim] = low.astype(out_ref.dtype)
+    out_ref[rim : rim + rows] = mask_ref[...]
+    out_ref[rim + rows :] = high.astype(out_ref.dtype)
+
+
+def grad_rims_kernel(grad_ref, out_ref, slots, send_sem, recv_sem):
+    rows, rim = out_ref.shape[0], slots.shape[1]
+    low, high = swap_rims(
+        grad_ref.at[pl.ds(0, rim)], grad_ref.at[pl.ds(rim + rows, rim)], slots, send_sem, recv_sem
+    )
+    out_ref[:rim] = grad_ref[rim : 2 * rim] + low
+    out_ref[rim:] = grad_ref[2 * rim : rim + rows] + high
+
+
+def rims_call(kernel, value, rows_out, collective_id, name):
+    vmem = pl.BlockSpec(memory_space=pltpu.VMEM)
+    return pl.pallas_call(
+        kernel,
+        out_shape=jax.ShapeDtypeStruct((rows_out, W), value.dtype),
+        in_specs=[vmem],
+        out_specs=vmem,
+        scratch_shapes=[
+            pltpu.VMEM((2, HALF + 1, W), value.dtype),
+            pltpu.SemaphoreType.DMA((2,)),
+            pltpu.SemaphoreType.DMA((2,)),
+        ],
+        compiler_params=pltpu.CompilerParams(collective_id=collective_id, has_side_effects=True),
+        name=name,
+    )(value)
 
 
 def exchange(n, source, slots, send_sem, recv_sem):
@@ -112,8 +169,8 @@
     def pad(x, low, high):
         return jnp.pad(x, ((0, 0), (0, 0), (low, high)))
 
-    row_fwd = pad(row, 0, rest)
-    row_adj = jnp.concatenate([row[..., :1], pad(row[..., :0:-1], rest, 0)], axis=-1)
+    row_fwd = pad(row, 1, rest - 1)
+    row_adj = pad(row[..., ::-1], rest, 0)
     col_fwd = pad(col[..., ::-1], rest, 0)
     col_adj = pad(col, rest, 0)
     return row_fwd, row_adj, col_fwd, col_adj
@@ -143,7 +200,9 @@
     target_ref, residual_ref, grad_ref, fields_ref,
 ):
     half = jnp.bfloat16
-    mask = mask_ref[...]
+    mask = mask_ref[...].astype(jnp.float32)
+    mask = jnp.concatenate([mask, jnp.zeros((mask.shape[0], LANES), jnp.float32)], axis=1)
+    mask = pltpu.roll(mask, 32, 1).astype(half)
 
     def forward_mode(k, intensity):
         row_taps = row_fwd_ref[k]
@@ -316,21 +375,9 @@
     mask = jnp.einsum(
         "pai,paj->ij", row_chosen.astype(jnp.bfloat16), spread, preferred_element_type=jnp.float32
     ).astype(jnp.bfloat16)
-    low, high = halo(mask, "tx", HALF)
-    padded = jnp.pad(
-        jnp.concatenate([low, mask, high], axis=0), ((0, 2 * rows_here - rows_here - 2 * HALF), (32, 96))
-    )
+    padded = rims_call(mask_rims_kernel, mask, 2 * rows_here, 2, "mask_rims")
     resist_residual, grad_padded = run_filters(padded, target, row_taps, col_taps, mode_weights)
-    count = devices
-    from_above = lax.ppermute(
-        grad_padded[HALF + rows_here : 2 * HALF + rows_here],
-        "tx",
-        [(i, i + 1) for i in range(count - 1)],
-    )
-    from_below = lax.ppermute(grad_padded[:HALF], "tx", [(i + 1, i) for i in range(count - 1)])
-    grad_mask = grad_padded[HALF : HALF + rows_here]
-    grad_mask = grad_mask + jnp.pad(from_above, ((0, rows_here - HALF), (0, 0)))
-    grad_mask = grad_mask + jnp.pad(from_below, ((rows_here - HALF, 0), (0, 0)))
+    grad_mask = rims_call(grad_rims_kernel, grad_padded, rows_here, 3, "grad_rims")
     row_rows = jnp.einsum(
         "pai,ij->paj", row_chosen.astype(jnp.float32), grad_mask, precision=lax.Precision.HIGHEST
     )

time: 69.4 us -> 76 us (1.095)
  Pallas kernels: 35.9 us -> 50.3 us
  starting transfers between devices: 10.3 us -> 0 us
  local copies, waits for them, and re-layouts: 5.15 us -> 9.64 us
  waiting for transfers between devices: 3.54 us -> 0 us
  matrix products: 9.43 us -> 10.9 us
    pallas_call x0 -> x2, Pallas kernels: none -> 14.1 us  [rims_call(): pl.pallas_call(kernel, out_shape=jax.ShapeDtypeStruct((rows_out, W), valu...]
    ppermute x4 -> x0, starting transfers between devices: 10.3 us -> none  [the longest x1 3.84 us: halo(): low = lax.ppermute(block[-width:], axis, forward)]
    ppermute x4 -> x0, waiting for transfers between devices: 3.54 us -> none  [the longest x1 2.59 us: halo(): high = lax.ppermute(block[:width], axis, backward)]
    pad x3 -> x4, local copies, waits for them, and re-layouts: 0.17 us -> 1.79 us  [pad(): return jnp.pad(x, ((0, 0), (0, 0), (low, high)))]
    unnamed x12, local copies, waits for them, and re-layouts: 0.04 us -> 1.51 us
    dot_general x1, matrix products: 1.84 us -> 2.67 us  [on_device(): jnp.einsum('pai,ij->paj', row_chosen.astype(jnp.float32), grad_mask, prec...]
  transfers between devices with their start and end apart: 4 -> 0, of which waited for: 2 -> 0; matrix products, arithmetic and copies ran while one was open for 3% -> 0% of each run, Pallas kernels for 0% -> 0%
where the time goes in v3:
time: 76 us; the launch traced here: 75.2 us
  Pallas kernels  50.3 us (66%)
  matrix products  10.9 us (14%)
  local copies, waits for them, and re-layouts  9.64 us (13%)
  other arithmetic  3.57 us (5%)
  between operations  0.84 us (1%)
    pallas_call x2, Pallas kernels, exchange_call(): pl.pallas_call(body, out_shape=jax.ShapeDtypeStruct(out_shape, value.dtyp...  19.9 us
    pallas_call x1, Pallas kernels, run_filters(): pl.pallas_call(body, out_shape=(jax.ShapeDtypeStruct((rows_here, W), jnp....  16.3 us
    pallas_call x2, Pallas kernels, rims_call(): pl.pallas_call(kernel, out_shape=jax.ShapeDtypeStruct((rows_out, W), valu...  14.1 us
    dot_general x1, matrix products, on_device(): jnp.einsum('paj,pcj->pac', row_rows, col_chosen.astype(jnp.float32), prec...  3.12 us
    dot_general x1, matrix products, on_device(): jnp.einsum('pai,paj->ij', row_chosen.astype(jnp.bfloat16), spread, prefer...  3 us
    dot_general x1, matrix products, on_device(): jnp.einsum('pai,ij->paj', row_chosen.astype(jnp.float32), grad_mask, prec...  2.67 us
    pad x4, local copies, waits for them, and re-layouts, pad(): return jnp.pad(x, ((0, 0), (0, 0), (low, high)))  1.79 us
    eq x1, local copies, waits for them, and re-layouts, on_device(): place_row[:, None, None] + offsets[None, :, None]  1.69 us

profile of v3, /device:TPU:1, one launch (start us, length us, event | category | flops | bytes accessed | tf_op | source)
XLA Modules:
  0.0 75.2 jit_solution(8590524860210158675)
XLA Ops:
  0.6 0.7 bitcast_add_fusion
  1.3 0.7 convert_element_type.40
  2.1 0.7 iota_add_fusion.1
  2.7 0.8 %pad.14.refs_1_ = f32[12,8,128]{2,1,0:T(8,128)S(1)} pad(bf16[12,8,63]{2,1,0:T(8,128)(2,1)} %bitcast.24, f32[]{:T(128)} %constant.4.clone.1), padding=0_0x0_0x1_64 | pad | bytes 61252 | tf_op jit(solution)/shard_map/jit(_pad)/pad | solution.py:170
  3.5 0.8 %rev.6 = f32[12,8,63]{2,1,0:T(8,128)S(1)} reverse(bf16[12,8,63]{2,1,0:T(8,128)(2,1)} %bitcast.25), dimensions={2} | reverse | bytes 36288 | tf_op jit(solution)/shard_map/rev | solution.py:173
  4.4 0.8 %rev.7 = f32[12,8,63]{2,1,0:T(8,128)S(1)} reverse(bf16[12,8,63]{2,1,0:T(8,128)(2,1)} %bitcast.26), dimensions={2} | reverse | bytes 36288 | tf_op jit(solution)/shard_map/rev | solution.py:174
  5.3 0.8 %pad.17.refs_4_ = f32[12,8,128]{2,1,0:T(8,128)S(1)} pad(bf16[12,8,63]{2,1,0:T(8,128)(2,1)} %bitcast.27, f32[]{:T(128)} %constant.4.clone.1), padding=0_0x0_0x65_0 | pad | bytes 61252 | tf_op jit(solution)/shard_map/jit(_pad)/pad | solution.py:170
  6.2 0.7 iota_add_fusion
  6.9 9.4 %gather_masters.1 = bf16[16,32,128]{2,1,0:T(8,128)(2,1)S(1)} custom-call(bf16[32,128]{1,0:T(8,128)(2,1)S(1)} %reshape.88.refs_0_), custom_call_target="tpu_custom_call" | custom-call | tf_op jit(solution)/shard_map/gather_masters/pallas_call | solution.py:147
  17.0 1.7 %copy.17 = pred[128,32,64]{2,1,0:T(32,128)(4,1)S(1)} copy(pred[128,32,64]{0,2,1:T(32,128)(4,1)S(1)} %iota_compare_fusion.3) | data formatting | bytes 524288 | tf_op jit(solution)/shard_map/eq | solution.py:354
  18.7 1.4 %copy.15 = bf16[128,32,32]{2,1,0:T(8,128)(2,1)S(1)} copy(bf16[128,32,32]{0,2,1:T(8,128)(2,1)S(1)} %bitcast.23) | data formatting | bytes 524288 | tf_op jit(solution)/shard_map/reshape | solution.py:367
  20.1 1.3 %fusion.1 = bf16[128,32,256]{2,1,0:T(8,128)(2,1)S(1)} fusion(bf16[128,32,32]{2,1,0:T(8,128)(2,1)S(1)} %copy.15, s32[128,32]{1,0:T(8,128)S(1)} %iota_add_fusion), kind=kOutput, calls=%fused_computation.3 | convolution fusion | flops 68157440 | bytes 2375680 | tf_op jit(solution)/shard_map/pab,pbj->paj/dot_general | solution.py:369
  21.5 3.0 %fusion.6.mask_ref = bf16[64,256]{1,0:T(8,128)(2,1)} fusion(bf16[128,32,256]{2,1,0:T(8,128)(2,1)S(1)} %fusion.1, s32[128,32]{0,1:T(8,128)S(1)} %iota_add_fusion.1), kind=kOutput, calls=%fused_computation.9 | convolution fusion | flops 134496256 | bytes 2146304 | tf_op jit(solution)/shard_map/pai,paj->ij/dot_general | solution.py:375
  24.5 6.6 %mask_rims.1.refs_5_ = bf16[128,256]{1,0:T(8,128)(2,1)} custom-call(bf16[64,256]{1,0:T(8,128)(2,1)} %fusion.6.mask_ref), custom_call_target="tpu_custom_call" | custom-call | tf_op jit(solution)/shard_map/mask_rims/pallas_call | solution.py:75
  31.1 0.8 %copy-done = bf16[128,256]{1,0:T(8,128)(2,1)S(1)} copy-done((bf16[128,256]{1,0:T(8,128)(2,1)S(1)}, bf16[128,256]{1,0:T(8,128)(2,1)}, u32[]{:S(2)}) %copy-start) | copy-done | bytes 65560
  31.9 16.3 %filters.1 = (f32[64,256]{1,0:T(8,128)}, f32[128,256]{1,0:T(8,128)S(1)}) custom-call(f32[12]{0:T(128)S(1)} %copy-done.3, f32[12,8,128]{2,1,0:T(8,128)S(1)} %pad.14.refs_1_, f32[12,8,128]{2,1,0:T(8,128)S(1)} %pad.15.refs_2_, f32[12,8,128]{2,1,0:T(8,128)S(1)} %pad.16.refs_3_, f32[12,8,128]{2,1,0:T(8,128)S(1)} %pad.17.refs_4_, bf16[128,256]{1,0:T(8,128)(2,1)S(1)} %copy-done, ...), custom_call_target="tpu_custom_call" | custom-call | tf_op jit(solution)/shard_map/filters/pallas_call | solution.py:310
  48.2 0.6 copy-done.1
  48.8 7.5 %grad_rims.1 = f32[64,256]{1,0:T(8,128)} custom-call(f32[128,256]{1,0:T(8,128)} %copy-done.1), custom_call_target="tpu_custom_call" | custom-call | tf_op jit(solution)/shard_map/grad_rims/pallas_call | solution.py:75
  56.3 2.7 %fusion.7 = f32[128,32,256]{2,1,0:T(8,128)S(1)} fusion(pred[128,32,64]{2,1,0:T(32,128)(4,1)S(1)} %copy.17, f32[64,256]{1,0:T(8,128)} %grad_rims.1), kind=kOutput, calls=%fused_computation.11 | convolution fusion | flops 805306368 | bytes 4521984 | tf_op jit(solution)/shard_map/pai,ij->paj/dot_general | solution.py:381
  59.0 3.1 %fusion = f32[128,32,32]{2,1,0:T(8,128)S(1)} fusion(f32[128,32,256]{2,1,0:T(8,128)S(1)} %fusion.7, s32[128,32]{1,0:T(8,128)S(1)} %iota_add_fusion), kind=kOutput, calls=%fused_computation.2 | convolution fusion | flops 403701760 | bytes 4734976 | tf_op jit(solution)/shard_map/paj,pcj->pac/dot_general | solution.py:384
  62.1 1.3 %copy.14 = f32[128,32,32]{0,2,1:T(8,128)S(1)} copy(f32[128,32,32]{2,1,0:T(8,128)S(1)} %fusion) | data formatting | bytes 1048576 | tf_op jit(solution)/shard_map/paj,pcj->pac/dot_general | solution.py:384
  63.4 0.5 fusion.10
  64.0 10.6 %sum_gradients.1 = f32[32,128]{1,0:T(8,128)S(1)} custom-call(f32[16,32,128]{2,1,0:T(8,128)S(1)} %reshape.92.refs_0_), custom_call_target="tpu_custom_call" | custom-call | tf_op jit(solution)/shard_map/sum_gradients/pallas_call | solution.py:147
  74.6 0.6 multiply_subtract_fusion
  (19 shorter events, 0.9 us)
Async XLA Ops:
  16.8 14.3 %copy-start.2 = (bf16[64,256]{1,0:T(8,128)(2,1)S(1)}, bf16[64,256]{1,0:T(8,128)(2,1)}, u32[]{:S(2)}) copy-start(bf16[64,256]{1,0:T(8,128)(2,1)} %refs_6_.1) | copy-start | bytes 98308
  16.8 14.3 %copy-start.3 = (f32[12]{0:T(128)S(1)}, f32[12]{0:T(128)}, u32[]{:S(2)}) copy-start(f32[12]{0:T(128)} %refs_0_.1) | copy-start | bytes 148
  31.1 0.8 %copy-start = (bf16[128,256]{1,0:T(8,128)(2,1)S(1)}, bf16[128,256]{1,0:T(8,128)(2,1)}, u32[]{:S(2)}) copy-start(bf16[128,256]{1,0:T(8,128)(2,1)} %mask_rims.1.refs_5_) | copy-start | bytes 196612
  48.2 0.6 copy-start.1
  59.0 15.6 %copy-start.4 = (f32[4,1024]{1,0:T(4,128)S(1)}, f32[4,1024]{1,0:T(4,128)}, u32[]{:S(2)}) copy-start(f32[4,1024]{1,0:T(4,128)} %param.10) | copy-start | bytes 49156
  59.0 15.6 %copy-start.5 = (f32[4,1024]{1,0:T(4,128)S(1)}, f32[4,1024]{1,0:T(4,128)}, u32[]{:S(2)}) copy-start(f32[4,1024]{1,0:T(4,128)} %param.11) | copy-start | bytes 49156

commit v4 on v2

--- a/solution.py
+++ b/solution.py
@@ -332,13 +332,13 @@
     grad_mask = grad_mask + jnp.pad(from_above, ((0, rows_here - HALF), (0, 0)))
     grad_mask = grad_mask + jnp.pad(from_below, ((rows_here - HALF, 0), (0, 0)))
     row_rows = jnp.einsum(
-        "pai,ij->paj", row_chosen.astype(jnp.float32), grad_mask, precision=lax.Precision.HIGHEST
+        "pai,ij->paj", row_chosen.astype(jnp.float32), grad_mask, precision=lax.Precision.HIGH
     )
     grad_patch = jnp.einsum(
-        "paj,pcj->pac", row_rows, col_chosen.astype(jnp.float32), precision=lax.Precision.HIGHEST
+        "paj,pcj->pac", row_rows, col_chosen.astype(jnp.float32), precision=lax.Precision.HIGH
     ).reshape(places, MS * MS)
     partial = jnp.dot(
-        chosen.astype(jnp.float32).T, grad_patch, precision=lax.Precision.HIGHEST
+        chosen.astype(jnp.float32).T, grad_patch, precision=lax.Precision.HIGH
     )
     master_grad = exchange_call(
         scatter_sum_kernel,

time: 69.4 us -> 67.6 us (0.974)
  matrix products: 9.43 us -> 7.93 us
    dot_general x1, matrix products: 3.12 us -> 2.3 us  [on_device(): jnp.einsum('paj,pcj->pac', row_rows, col_chosen.astype(jnp.float32), prec...]
where the time goes in v4:
time: 67.6 us; the launch traced here: 67.3 us
  Pallas kernels  35.7 us (53%)
  starting transfers between devices  10.1 us (15%)
  matrix products  7.93 us (12%)
  local copies, waits for them, and re-layouts  5.15 us (8%)
  other arithmetic  3.76 us (6%)
  waiting for transfers between devices  3.72 us (6%)
  between operations  0.92 us (1%)
    pallas_call x2, Pallas kernels, exchange_call(): pl.pallas_call(body, out_shape=jax.ShapeDtypeStruct(out_shape, value.dtyp...  19.5 us
    pallas_call x1, Pallas kernels, run_filters(): pl.pallas_call(body, out_shape=(jax.ShapeDtypeStruct((rows_here, W), jnp....  16.2 us
    ppermute x1, starting transfers between devices, halo(): low = lax.ppermute(block[-width:], axis, forward)  3.84 us
    ppermute x1, waiting for transfers between devices, halo(): high = lax.ppermute(block[:width], axis, backward)  2.59 us
    ppermute x1, starting transfers between devices, on_device(): lax.ppermute(grad_padded[:HALF], 'tx', [(i + 1, i) for i in range(count -...  2.4 us
    dot_general x1, matrix products, on_device(): jnp.einsum('pai,paj->ij', row_chosen.astype(jnp.bfloat16), spread, prefer...  2.38 us
    dot_general x1, matrix products, on_device(): jnp.einsum('paj,pcj->pac', row_rows, col_chosen.astype(jnp.float32), prec...  2.3 us
    ppermute x1, starting transfers between devices, on_device(): lax.ppermute(grad_padded[HALF + rows_here:2 * HALF + rows_here], 'tx', [(...  1.92 us
  transfers between devices with their start and end apart: 4, of which 2 were waited for; matrix products, arithmetic and copies ran while one was open for 3% of the time, Pallas kernels for 0%

profile of v4, /device:TPU:1, one launch (start us, length us, event | category | flops | bytes accessed | tf_op | source)
XLA Modules:
  0.0 67.3 jit_solution(4945341886488889140)
XLA Ops:
  0.6 0.7 %convert_element_type.47 = bf16[4,1024]{1,0:T(4,128)(2,1)S(1)} convert(f32[4,1024]{1,0:T(4,128)} %param.10) | non-fusion elementwise | flops 4096 | bytes 24576 | tf_op jit(solution)/shard_map/convert_element_type | solution.py:285
  1.4 0.7 iota_add_fusion.1
  2.0 0.7 %iota_add_fusion = s32[128,32]{1,0:T(8,128)S(1)} fusion(s32[128]{0:T(128)} %param.15), kind=kLoop, calls=%fused_computation.32 | loop fusion | flops 4096 | bytes 16896 | tf_op jit(solution)/shard_map/add | solution.py:299
  2.8 9.4 %gather_masters.1 = bf16[16,32,128]{2,1,0:T(8,128)(2,1)S(1)} custom-call(bf16[32,128]{1,0:T(8,128)(2,1)S(1)} %reshape.88.refs_0_), custom_call_target="tpu_custom_call" | custom-call | tf_op jit(solution)/shard_map/gather_masters/pallas_call | solution.py:90
  12.2 0.7 %bitcast_add_fusion = (s32[128]{0:T(128)S(1)}, s32[128]{0:T(128)S(1)}) fusion(s32[128]{0:T(128)} %param.13, s32[128,1]{0,1:T(1,128)} %param.12, s32[]{:T(128)S(6)} %axis_index.12), kind=kLoop, calls=%fused_computation.48 | loop fusion | flops 1536 | bytes 2052 | tf_op jit(solution)/shard_map/add | solution.py:290
  12.9 0.3 convolution_convert_fusion
  13.2 0.2 copy.13
  13.4 1.4 %copy.15 = bf16[128,32,32]{2,1,0:T(8,128)(2,1)S(1)} copy(bf16[128,32,32]{0,2,1:T(8,128)(2,1)S(1)} %bitcast.23) | data formatting | bytes 524288 | tf_op jit(solution)/shard_map/reshape | solution.py:308
  14.8 1.3 %fusion.1 = bf16[128,32,256]{2,1,0:T(8,128)(2,1)S(1)} fusion(bf16[128,32,32]{2,1,0:T(8,128)(2,1)S(1)} %copy.15, s32[128,32]{1,0:T(8,128)S(1)} %iota_add_fusion), kind=kOutput, calls=%fused_computation.3 | convolution fusion | flops 68157440 | bytes 2375680 | tf_op jit(solution)/shard_map/pab,pbj->paj/dot_general | solution.py:310
  16.2 2.4 %fusion.6 = bf16[64,256]{1,0:T(8,128)(2,1)S(1)} fusion(bf16[128,32,256]{2,1,0:T(8,128)(2,1)S(1)} %fusion.1, s32[128,32]{0,1:T(8,128)S(1)} %iota_add_fusion.1), kind=kOutput, calls=%fused_computation.9 | convolution fusion | flops 134496256 | bytes 2146304 | tf_op jit(solution)/shard_map/pai,paj->ij/dot_general | solution.py:316
  18.6 3.8 %collective-permute-start = (bf16[31,256]{1,0:T(8,128)(2,1)S(1)}, bf16[31,256]{1,0:T(8,128)(2,1)S(1)}, u32[]{:S(2)}, u32[]{:S(2)}) collective-permute-start(bf16[31,256]{1,0:T(8,128)(2,1)S(1)} %get-tuple-element.11), channel_id=1, source_target_pairs={{0,1},{1,2},{2,3},{3,4},{4,5},{5,6},{6,7},{7,8},{8,9},{9,10},{10,1... | collective-permute-start | bytes 47624 | tf_op jit(solution)/shard_map/ppermute | solution.py:28
  22.4 1.9 %collective-permute-start.1 = (bf16[31,256]{1,0:T(8,128)(2,1)S(1)}, bf16[31,256]{1,0:T(8,128)(2,1)S(1)}, u32[]{:S(2)}, u32[]{:S(2)}) collective-permute-start(bf16[31,256]{1,0:T(8,128)(2,1)S(1)} %get-tuple-element.12), channel_id=1, source_target_pairs={{1,0},{2,1},{3,2},{4,3},{5,4},{6,5},{7,6},{8,7},{9,8},{10,9},{11,1... | collective-permute-start | bytes 47624 | tf_op jit(solution)/shard_map/ppermute | solution.py:29
  24.9 2.6 %collective-permute-done.1 = bf16[31,256]{1,0:T(8,128)(2,1)S(1)} collective-permute-done((bf16[31,256]{1,0:T(8,128)(2,1)S(1)}, bf16[31,256]{1,0:T(8,128)(2,1)S(1)}, u32[]{:S(2)}, u32[]{:S(2)}) %collective-permute-start.1) | collective-permute-done | bytes 15904 | tf_op jit(solution)/shard_map/ppermute | solution.py:29
  27.6 16.2 %filters.1 = (f32[64,256]{1,0:T(8,128)}, f32[128,256]{1,0:T(8,128)S(1)}) custom-call(f32[12]{0:T(128)S(1)} %copy-done.1, f32[12,8,128]{2,1,0:T(8,128)S(1)} %pad.27.refs_1_, f32[12,8,128]{2,1,0:T(8,128)S(1)} %select_maximum_fusion.refs_2_, f32[12,8,128]{2,1,0:T(8,128)S(1)} %pad.29.refs_3_, f32[12,8,128]{2,1,0:T(8,128)S(1)} %pad.30.refs_4_, ...), custom_call_target="tpu_custom_call" | custom-call | tf_op jit(solution)/shard_map/filters/pallas_call | solution.py:251
  43.8 1.9 %collective-permute-start.2 = (f32[31,256]{1,0:T(8,128)S(1)}, f32[31,256]{1,0:T(8,128)S(1)}, u32[]{:S(2)}, u32[]{:S(2)}) collective-permute-start(f32[31,256]{1,0:T(8,128)S(1)} %get-tuple-element.9), channel_id=1, source_target_pairs={{0,1},{1,2},{2,3},{3,4},{4,5},{5,6},{6,7},{7,8},{8,9},{9,10},{10,1... | collective-permute-start | bytes 95240 | tf_op jit(solution)/shard_map/ppermute | solution.py:325
  45.8 2.4 %collective-permute-start.3 = (f32[31,256]{1,0:T(8,128)S(1)}, f32[31,256]{1,0:T(8,128)S(1)}, u32[]{:S(2)}, u32[]{:S(2)}) collective-permute-start(f32[31,256]{1,0:T(8,128)S(1)} %get-tuple-element.10), channel_id=1, source_target_pairs={{1,0},{2,1},{3,2},{4,3},{5,4},{6,5},{7,6},{8,7},{9,8},{10,9},{11,1... | collective-permute-start | bytes 95240 | tf_op jit(solution)/shard_map/ppermute | solution.py:330
  48.3 1.7 %copy.17 = pred[128,32,64]{2,1,0:T(32,128)(4,1)S(1)} copy(pred[128,32,64]{0,2,1:T(32,128)(4,1)S(1)} %iota_compare_fusion.3) | data formatting | bytes 524288 | tf_op jit(solution)/shard_map/eq | solution.py:295
  50.0 1.1 %collective-permute-done.3 = f32[31,256]{1,0:T(8,128)S(1)} collective-permute-done((f32[31,256]{1,0:T(8,128)S(1)}, f32[31,256]{1,0:T(8,128)S(1)}, u32[]{:S(2)}, u32[]{:S(2)}) %collective-permute-start.3) | collective-permute-done | bytes 31776 | tf_op jit(solution)/shard_map/ppermute | solution.py:330
  51.2 1.2 %fusion.17 = f32[128,32,256]{2,1,0:T(8,128)S(1)} fusion(pred[128,32,64]{2,1,0:T(32,128)(4,1)S(1)} %copy.17, f32[31,256]{1,0:T(8,128)S(1)} %collective-permute-done.3, f32[31,256]{1,0:T(8,128)S(1)} %collective-permute-done.2, f32[128,256]{1,0:T(8,128)S(1)} %get-tuple-element.6), kind=kOutput, calls=%fused_computation.24 | convolution fusion | flops 402685952 | bytes 4849664 | tf_op jit(solution)/shard_map/pai,ij->paj/dot_general | solution.py:334
  52.4 2.3 %fusion = f32[128,32,32]{2,1,0:T(8,128)S(1)} fusion(f32[128,32,256]{2,1,0:T(8,128)S(1)} %fusion.17, s32[128,32]{1,0:T(8,128)S(1)} %iota_add_fusion), kind=kOutput, calls=%fused_computation.2 | convolution fusion | flops 202375168 | bytes 4734976 | tf_op jit(solution)/shard_map/paj,pcj->pac/dot_general | solution.py:337
  54.7 1.3 %copy.14 = f32[128,32,32]{0,2,1:T(8,128)S(1)} copy(f32[128,32,32]{2,1,0:T(8,128)S(1)} %fusion) | data formatting | bytes 1048576 | tf_op jit(solution)/shard_map/paj,pcj->pac/dot_general | solution.py:337
  56.0 0.4 fusion.25
  56.5 10.2 %sum_gradients.1 = f32[32,128]{1,0:T(8,128)S(1)} custom-call(f32[16,32,128]{2,1,0:T(8,128)S(1)} %reshape.92.refs_0_), custom_call_target="tpu_custom_call" | custom-call | tf_op jit(solution)/shard_map/sum_gradients/pallas_call | solution.py:90
  66.7 0.6 multiply_subtract_fusion
  (30 shorter events, 0.9 us)
Async XLA Ops:
  12.1 12.2 %copy-start.2 = (bf16[12,4,2,63]{3,2,1,0:T(2,128)(2,1)S(1)}, bf16[12,4,2,63]{3,2,1,0:T(2,128)(2,1)}, u32[]{:S(2)}) copy-start(bf16[12,4,2,63]{3,2,1,0:T(2,128)(2,1)} %param.16) | copy-start | bytes 36292
  13.2 11.4 %copy-start.3 = (bf16[12,4,2,63]{3,2,1,0:T(2,128)(2,1)S(1)}, bf16[12,4,2,63]{3,2,1,0:T(2,128)(2,1)}, u32[]{:S(2)}) copy-start(bf16[12,4,2,63]{3,2,1,0:T(2,128)(2,1)} %param.17) | copy-start | bytes 36292
  13.4 14.2 %copy-start = (bf16[64,256]{1,0:T(8,128)(2,1)S(1)}, bf16[64,256]{1,0:T(8,128)(2,1)}, u32[]{:S(2)}) copy-start(bf16[64,256]{1,0:T(8,128)(2,1)} %refs_6_.1) | copy-start | bytes 98308
  13.4 14.2 %copy-start.1 = (f32[12]{0:T(128)S(1)}, f32[12]{0:T(128)}, u32[]{:S(2)}) copy-start(f32[12]{0:T(128)} %refs_0_.1) | copy-start | bytes 148
  18.6 6.3 %collective-permute-start = (bf16[31,256]{1,0:T(8,128)(2,1)S(1)}, bf16[31,256]{1,0:T(8,128)(2,1)S(1)}, u32[]{:S(2)}, u32[]{:S(2)}) collective-permute-start(bf16[31,256]{1,0:T(8,128)(2,1)S(1)} %get-tuple-element.11), channel_id=1, source_target_pairs={{0,1},{1,2},{2,3},{3,4},{4,5},{5,6},{6,7},{7,8},{8,9},{9,10},{10,1... | collective-permute-start | bytes 47624 | tf_op jit(solution)/shard_map/ppermute | solution.py:28
  22.4 5.1 %collective-permute-start.1 = (bf16[31,256]{1,0:T(8,128)(2,1)S(1)}, bf16[31,256]{1,0:T(8,128)(2,1)S(1)}, u32[]{:S(2)}, u32[]{:S(2)}) collective-permute-start(bf16[31,256]{1,0:T(8,128)(2,1)S(1)} %get-tuple-element.12), channel_id=1, source_target_pairs={{1,0},{2,1},{3,2},{4,3},{5,4},{6,5},{7,6},{8,7},{9,8},{10,9},{11,1... | collective-permute-start | bytes 47624 | tf_op jit(solution)/shard_map/ppermute | solution.py:29
  43.8 6.2 %collective-permute-start.2 = (f32[31,256]{1,0:T(8,128)S(1)}, f32[31,256]{1,0:T(8,128)S(1)}, u32[]{:S(2)}, u32[]{:S(2)}) collective-permute-start(f32[31,256]{1,0:T(8,128)S(1)} %get-tuple-element.9), channel_id=1, source_target_pairs={{0,1},{1,2},{2,3},{3,4},{4,5},{5,6},{6,7},{7,8},{8,9},{9,10},{10,1... | collective-permute-start | bytes 95240 | tf_op jit(solution)/shard_map/ppermute | solution.py:325
  45.8 5.4 %collective-permute-start.3 = (f32[31,256]{1,0:T(8,128)S(1)}, f32[31,256]{1,0:T(8,128)S(1)}, u32[]{:S(2)}, u32[]{:S(2)}) collective-permute-start(f32[31,256]{1,0:T(8,128)S(1)} %get-tuple-element.10), channel_id=1, source_target_pairs={{1,0},{2,1},{3,2},{4,3},{5,4},{6,5},{7,6},{8,7},{9,8},{10,9},{11,1... | collective-permute-start | bytes 95240 | tf_op jit(solution)/shard_map/ppermute | solution.py:330
  52.4 14.3 %copy-start.4 = (f32[4,1024]{1,0:T(4,128)S(1)}, f32[4,1024]{1,0:T(4,128)}, u32[]{:S(2)}) copy-start(f32[4,1024]{1,0:T(4,128)} %param.10) | copy-start | bytes 49156
  52.4 14.3 %copy-start.5 = (f32[4,1024]{1,0:T(4,128)S(1)}, f32[4,1024]{1,0:T(4,128)}, u32[]{:S(2)}) copy-start(f32[4,1024]{1,0:T(4,128)} %param.11) | copy-start | bytes 49156

commit v5 on v4

--- a/solution.py
+++ b/solution.py
@@ -172,7 +172,7 @@
         return intensity + weights_ref[k] * (re * re + im * im)
 
     intensity = lax.fori_loop(
-        0, MODES, forward_mode, jnp.zeros((2 * rows_here, LANES), jnp.float32)
+        0, MODES, forward_mode, jnp.zeros((2 * rows_here, LANES), jnp.float32), unroll=2
     )
     resist = 1.0 / (1.0 + jnp.exp(-(steepness * (intensity - threshold))))
     target = target_ref[...].astype(jnp.float32)
@@ -237,7 +237,7 @@
         grad_ref[...] += jnp.dot(row_band, stacked, preferred_element_type=jnp.float32)
         return carry
 
-    lax.fori_loop(0, MODES, adjoint_mode, 0)
+    lax.fori_loop(0, MODES, adjoint_mode, 0, unroll=2)
 
 
 def run_filters(mask, target, row_taps, col_taps, mode_weights):

time: 67.6 us -> 62.4 us (0.923)
  Pallas kernels: 35.7 us -> 30.5 us
    pallas_call x1, Pallas kernels: 16.2 us -> 11 us  [run_filters(): pl.pallas_call(body, out_shape=(jax.ShapeDtypeStruct((rows_here, W), jnp....]
  transfers between devices with their start and end apart: 4 -> 4, of which waited for: 2 -> 2; matrix products, arithmetic and copies ran while one was open for 3% -> 4% of each run, Pallas kernels for 0% -> 0%
where the time goes in v5:
time: 62.4 us; the launch traced here: 62.1 us
  Pallas kernels  30.5 us (49%)
  starting transfers between devices  10.1 us (16%)
  matrix products  7.93 us (13%)
  local copies, waits for them, and re-layouts  5.15 us (8%)
  other arithmetic  3.76 us (6%)
  waiting for transfers between devices  3.72 us (6%)
  between operations  0.92 us (1%)
    pallas_call x2, Pallas kernels, exchange_call(): pl.pallas_call(body, out_shape=jax.ShapeDtypeStruct(out_shape, value.dtyp...  19.5 us
    pallas_call x1, Pallas kernels, run_filters(): pl.pallas_call(body, out_shape=(jax.ShapeDtypeStruct((rows_here, W), jnp....  11 us
    ppermute x1, starting transfers between devices, halo(): low = lax.ppermute(block[-width:], axis, forward)  3.84 us
    ppermute x1, waiting for transfers between devices, halo(): high = lax.ppermute(block[:width], axis, backward)  2.59 us
    ppermute x1, starting transfers between devices, on_device(): lax.ppermute(grad_padded[:HALF], 'tx', [(i + 1, i) for i in range(count -...  2.4 us
    dot_general x1, matrix products, on_device(): jnp.einsum('pai,paj->ij', row_chosen.astype(jnp.bfloat16), spread, prefer...  2.38 us
    dot_general x1, matrix products, on_device(): jnp.einsum('paj,pcj->pac', row_rows, col_chosen.astype(jnp.float32), prec...  2.3 us
    ppermute x1, starting transfers between devices, on_device(): lax.ppermute(grad_padded[HALF + rows_here:2 * HALF + rows_here], 'tx', [(...  1.92 us
  transfers between devices with their start and end apart: 4, of which 2 were waited for; matrix products, arithmetic and copies ran while one was open for 4% of the time, Pallas kernels for 0%

profile of v5, /device:TPU:1, one launch (start us, length us, event | category | flops | bytes accessed | tf_op | source)
XLA Modules:
  0.0 62.1 jit_solution(15228701824247144808)
XLA Ops:
  0.6 0.7 %convert_element_type.47 = bf16[4,1024]{1,0:T(4,128)(2,1)S(1)} convert(f32[4,1024]{1,0:T(4,128)} %param.10) | non-fusion elementwise | flops 4096 | bytes 24576 | tf_op jit(solution)/shard_map/convert_element_type | solution.py:285
  1.4 0.7 %iota_add_fusion.1 = s32[128,32]{0,1:T(8,128)S(1)} fusion(s32[128]{0:T(128)} %param.14), kind=kLoop, calls=%fused_computation.42 | loop fusion | flops 4096 | bytes 16896 | tf_op jit(solution)/shard_map/add | solution.py:295
  2.0 0.7 %iota_add_fusion = s32[128,32]{1,0:T(8,128)S(1)} fusion(s32[128]{0:T(128)} %param.15), kind=kLoop, calls=%fused_computation.32 | loop fusion | flops 4096 | bytes 16896 | tf_op jit(solution)/shard_map/add | solution.py:299
  2.8 9.4 %gather_masters.1 = bf16[16,32,128]{2,1,0:T(8,128)(2,1)S(1)} custom-call(bf16[32,128]{1,0:T(8,128)(2,1)S(1)} %reshape.88.refs_0_), custom_call_target="tpu_custom_call" | custom-call | tf_op jit(solution)/shard_map/gather_masters/pallas_call | solution.py:90
  12.2 0.7 %bitcast_add_fusion = (s32[128]{0:T(128)S(1)}, s32[128]{0:T(128)S(1)}) fusion(s32[128]{0:T(128)} %param.13, s32[128,1]{0,1:T(1,128)} %param.12, s32[]{:T(128)S(6)} %axis_index.12), kind=kLoop, calls=%fused_computation.48 | loop fusion | flops 1536 | bytes 2052 | tf_op jit(solution)/shard_map/add | solution.py:290
  12.9 0.3 convolution_convert_fusion
  13.2 0.2 copy.13
  13.4 1.4 %copy.15 = bf16[128,32,32]{2,1,0:T(8,128)(2,1)S(1)} copy(bf16[128,32,32]{0,2,1:T(8,128)(2,1)S(1)} %bitcast.23) | data formatting | bytes 524288 | tf_op jit(solution)/shard_map/reshape | solution.py:308
  14.8 1.3 %fusion.1 = bf16[128,32,256]{2,1,0:T(8,128)(2,1)S(1)} fusion(bf16[128,32,32]{2,1,0:T(8,128)(2,1)S(1)} %copy.15, s32[128,32]{1,0:T(8,128)S(1)} %iota_add_fusion), kind=kOutput, calls=%fused_computation.3 | convolution fusion | flops 68157440 | bytes 2375680 | tf_op jit(solution)/shard_map/pab,pbj->paj/dot_general | solution.py:310
  16.2 2.4 %fusion.6 = bf16[64,256]{1,0:T(8,128)(2,1)S(1)} fusion(bf16[128,32,256]{2,1,0:T(8,128)(2,1)S(1)} %fusion.1, s32[128,32]{0,1:T(8,128)S(1)} %iota_add_fusion.1), kind=kOutput, calls=%fused_computation.9 | convolution fusion | flops 134496256 | bytes 2146304 | tf_op jit(solution)/shard_map/pai,paj->ij/dot_general | solution.py:316
  18.6 3.8 %collective-permute-start = (bf16[31,256]{1,0:T(8,128)(2,1)S(1)}, bf16[31,256]{1,0:T(8,128)(2,1)S(1)}, u32[]{:S(2)}, u32[]{:S(2)}) collective-permute-start(bf16[31,256]{1,0:T(8,128)(2,1)S(1)} %get-tuple-element.11), channel_id=1, source_target_pairs={{0,1},{1,2},{2,3},{3,4},{4,5},{5,6},{6,7},{7,8},{8,9},{9,10},{10,1... | collective-permute-start | bytes 47624 | tf_op jit(solution)/shard_map/ppermute | solution.py:28
  22.4 1.9 %collective-permute-start.1 = (bf16[31,256]{1,0:T(8,128)(2,1)S(1)}, bf16[31,256]{1,0:T(8,128)(2,1)S(1)}, u32[]{:S(2)}, u32[]{:S(2)}) collective-permute-start(bf16[31,256]{1,0:T(8,128)(2,1)S(1)} %get-tuple-element.12), channel_id=1, source_target_pairs={{1,0},{2,1},{3,2},{4,3},{5,4},{6,5},{7,6},{8,7},{9,8},{10,9},{11,1... | collective-permute-start | bytes 47624 | tf_op jit(solution)/shard_map/ppermute | solution.py:29
  24.9 2.6 %collective-permute-done.1 = bf16[31,256]{1,0:T(8,128)(2,1)S(1)} collective-permute-done((bf16[31,256]{1,0:T(8,128)(2,1)S(1)}, bf16[31,256]{1,0:T(8,128)(2,1)S(1)}, u32[]{:S(2)}, u32[]{:S(2)}) %collective-permute-start.1) | collective-permute-done | bytes 15904 | tf_op jit(solution)/shard_map/ppermute | solution.py:29
  27.6 11.0 %filters.1 = (f32[64,256]{1,0:T(8,128)}, f32[128,256]{1,0:T(8,128)S(1)}) custom-call(f32[12]{0:T(128)S(1)} %copy-done.1, f32[12,8,128]{2,1,0:T(8,128)S(1)} %pad.27.refs_1_, f32[12,8,128]{2,1,0:T(8,128)S(1)} %select_maximum_fusion.refs_2_, f32[12,8,128]{2,1,0:T(8,128)S(1)} %pad.29.refs_3_, f32[12,8,128]{2,1,0:T(8,128)S(1)} %pad.30.refs_4_, ...), custom_call_target="tpu_custom_call" | custom-call | tf_op jit(solution)/shard_map/filters/pallas_call | solution.py:251
  38.6 1.9 %collective-permute-start.2 = (f32[31,256]{1,0:T(8,128)S(1)}, f32[31,256]{1,0:T(8,128)S(1)}, u32[]{:S(2)}, u32[]{:S(2)}) collective-permute-start(f32[31,256]{1,0:T(8,128)S(1)} %get-tuple-element.9), channel_id=1, source_target_pairs={{0,1},{1,2},{2,3},{3,4},{4,5},{5,6},{6,7},{7,8},{8,9},{9,10},{10,1... | collective-permute-start | bytes 95240 | tf_op jit(solution)/shard_map/ppermute | solution.py:325
  40.5 2.4 %collective-permute-start.3 = (f32[31,256]{1,0:T(8,128)S(1)}, f32[31,256]{1,0:T(8,128)S(1)}, u32[]{:S(2)}, u32[]{:S(2)}) collective-permute-start(f32[31,256]{1,0:T(8,128)S(1)} %get-tuple-element.10), channel_id=1, source_target_pairs={{1,0},{2,1},{3,2},{4,3},{5,4},{6,5},{7,6},{8,7},{9,8},{10,9},{11,1... | collective-permute-start | bytes 95240 | tf_op jit(solution)/shard_map/ppermute | solution.py:330
  43.1 1.7 %copy.17 = pred[128,32,64]{2,1,0:T(32,128)(4,1)S(1)} copy(pred[128,32,64]{0,2,1:T(32,128)(4,1)S(1)} %iota_compare_fusion.3) | data formatting | bytes 524288 | tf_op jit(solution)/shard_map/eq | solution.py:295
  44.8 1.1 %collective-permute-done.3 = f32[31,256]{1,0:T(8,128)S(1)} collective-permute-done((f32[31,256]{1,0:T(8,128)S(1)}, f32[31,256]{1,0:T(8,128)S(1)}, u32[]{:S(2)}, u32[]{:S(2)}) %collective-permute-start.3) | collective-permute-done | bytes 31776 | tf_op jit(solution)/shard_map/ppermute | solution.py:330
  45.9 1.2 %fusion.17 = f32[128,32,256]{2,1,0:T(8,128)S(1)} fusion(pred[128,32,64]{2,1,0:T(32,128)(4,1)S(1)} %copy.17, f32[31,256]{1,0:T(8,128)S(1)} %collective-permute-done.3, f32[31,256]{1,0:T(8,128)S(1)} %collective-permute-done.2, f32[128,256]{1,0:T(8,128)S(1)} %get-tuple-element.6), kind=kOutput, calls=%fused_computation.24 | convolution fusion | flops 402685952 | bytes 4849664 | tf_op jit(solution)/shard_map/pai,ij->paj/dot_general | solution.py:334
  47.2 2.3 %fusion = f32[128,32,32]{2,1,0:T(8,128)S(1)} fusion(f32[128,32,256]{2,1,0:T(8,128)S(1)} %fusion.17, s32[128,32]{1,0:T(8,128)S(1)} %iota_add_fusion), kind=kOutput, calls=%fused_computation.2 | convolution fusion | flops 202375168 | bytes 4734976 | tf_op jit(solution)/shard_map/paj,pcj->pac/dot_general | solution.py:337
  49.5 1.3 %copy.14 = f32[128,32,32]{0,2,1:T(8,128)S(1)} copy(f32[128,32,32]{2,1,0:T(8,128)S(1)} %fusion) | data formatting | bytes 1048576 | tf_op jit(solution)/shard_map/paj,pcj->pac/dot_general | solution.py:337
  50.8 0.4 fusion.25
  51.2 10.2 %sum_gradients.1 = f32[32,128]{1,0:T(8,128)S(1)} custom-call(f32[16,32,128]{2,1,0:T(8,128)S(1)} %reshape.92.refs_0_), custom_call_target="tpu_custom_call" | custom-call | tf_op jit(solution)/shard_map/sum_gradients/pallas_call | solution.py:90
  61.4 0.6 %multiply_subtract_fusion = (f32[4,1024]{1,0:T(4,128)}, f32[4,1024]{1,0:T(4,128)}) fusion(f32[4,1024]{1,0:T(4,128)S(1)} %copy-done.4, f32[4,1024]{1,0:T(4,128)S(1)} %reshape.93, f32[4,1024]{1,0:T(4,128)S(1)} %copy-done.5), kind=kLoop, calls=%fused_computation.40 | loop fusion | flops 16384 | bytes 81920 | tf_op jit(solution)/shard_map/sub | solution.py:352
  (30 shorter events, 0.9 us)
Async XLA Ops:
  12.1 12.2 %copy-start.2 = (bf16[12,4,2,63]{3,2,1,0:T(2,128)(2,1)S(1)}, bf16[12,4,2,63]{3,2,1,0:T(2,128)(2,1)}, u32[]{:S(2)}) copy-start(bf16[12,4,2,63]{3,2,1,0:T(2,128)(2,1)} %param.16) | copy-start | bytes 36292
  13.2 11.4 %copy-start.3 = (bf16[12,4,2,63]{3,2,1,0:T(2,128)(2,1)S(1)}, bf16[12,4,2,63]{3,2,1,0:T(2,128)(2,1)}, u32[]{:S(2)}) copy-start(bf16[12,4,2,63]{3,2,1,0:T(2,128)(2,1)} %param.17) | copy-start | bytes 36292
  13.4 14.2 %copy-start = (bf16[64,256]{1,0:T(8,128)(2,1)S(1)}, bf16[64,256]{1,0:T(8,128)(2,1)}, u32[]{:S(2)}) copy-start(bf16[64,256]{1,0:T(8,128)(2,1)} %refs_6_.1) | copy-start | bytes 98308
  13.4 14.2 %copy-start.1 = (f32[12]{0:T(128)S(1)}, f32[12]{0:T(128)}, u32[]{:S(2)}) copy-start(f32[12]{0:T(128)} %refs_0_.1) | copy-start | bytes 148
  18.6 6.3 %collective-permute-start = (bf16[31,256]{1,0:T(8,128)(2,1)S(1)}, bf16[31,256]{1,0:T(8,128)(2,1)S(1)}, u32[]{:S(2)}, u32[]{:S(2)}) collective-permute-start(bf16[31,256]{1,0:T(8,128)(2,1)S(1)} %get-tuple-element.11), channel_id=1, source_target_pairs={{0,1},{1,2},{2,3},{3,4},{4,5},{5,6},{6,7},{7,8},{8,9},{9,10},{10,1... | collective-permute-start | bytes 47624 | tf_op jit(solution)/shard_map/ppermute | solution.py:28
  22.4 5.1 %collective-permute-start.1 = (bf16[31,256]{1,0:T(8,128)(2,1)S(1)}, bf16[31,256]{1,0:T(8,128)(2,1)S(1)}, u32[]{:S(2)}, u32[]{:S(2)}) collective-permute-start(bf16[31,256]{1,0:T(8,128)(2,1)S(1)} %get-tuple-element.12), channel_id=1, source_target_pairs={{1,0},{2,1},{3,2},{4,3},{5,4},{6,5},{7,6},{8,7},{9,8},{10,9},{11,1... | collective-permute-start | bytes 47624 | tf_op jit(solution)/shard_map/ppermute | solution.py:29
  38.6 6.2 %collective-permute-start.2 = (f32[31,256]{1,0:T(8,128)S(1)}, f32[31,256]{1,0:T(8,128)S(1)}, u32[]{:S(2)}, u32[]{:S(2)}) collective-permute-start(f32[31,256]{1,0:T(8,128)S(1)} %get-tuple-element.9), channel_id=1, source_target_pairs={{0,1},{1,2},{2,3},{3,4},{4,5},{5,6},{6,7},{7,8},{8,9},{9,10},{10,1... | collective-permute-start | bytes 95240 | tf_op jit(solution)/shard_map/ppermute | solution.py:325
  40.5 5.4 %collective-permute-start.3 = (f32[31,256]{1,0:T(8,128)S(1)}, f32[31,256]{1,0:T(8,128)S(1)}, u32[]{:S(2)}, u32[]{:S(2)}) collective-permute-start(f32[31,256]{1,0:T(8,128)S(1)} %get-tuple-element.10), channel_id=1, source_target_pairs={{1,0},{2,1},{3,2},{4,3},{5,4},{6,5},{7,6},{8,7},{9,8},{10,9},{11,1... | collective-permute-start | bytes 95240 | tf_op jit(solution)/shard_map/ppermute | solution.py:330
  47.2 14.3 %copy-start.4 = (f32[4,1024]{1,0:T(4,128)S(1)}, f32[4,1024]{1,0:T(4,128)}, u32[]{:S(2)}) copy-start(f32[4,1024]{1,0:T(4,128)} %param.10) | copy-start | bytes 49156
  47.2 14.3 %copy-start.5 = (f32[4,1024]{1,0:T(4,128)S(1)}, f32[4,1024]{1,0:T(4,128)}, u32[]{:S(2)}) copy-start(f32[4,1024]{1,0:T(4,128)} %param.11) | copy-start | bytes 49156
